TPU v7x, 32 devices: a whole 2x2x4 slice. The times are simulated.
32 devices in a mesh: dp: 4 (over y, x), blk: 8 (over z, core).
Axes of the slice: x: 2, y: 2, z: 4, core: 2. Of those that a mesh axis runs over, the one named last changes fastest.
Arguments:
- tokens: bfloat16 [8, 512, 1024], P('dp', 'blk'), may hold values from -6 to 6
- doc_ids: int32 [8, 512], P('dp', 'blk'), may hold values from 0 to 7, as said below
- w_query: float32 [1024, 1024], P(('dp', 'blk')), may hold values from -0.1875 to 0.1875
- w_key: float32 [1024, 1024], P(('dp', 'blk')), may hold values from -0.1875 to 0.1875
- w_value: float32 [1024, 1024], P(('dp', 'blk')), may hold values from -0.1875 to 0.1875
- w_out: float32 [1024, 1024], P(('dp', 'blk')), may hold values from -0.1875 to 0.1875
- w_up: float32 [1024, 4096], P(('dp', 'blk')), may hold values from -0.1875 to 0.1875
- w_gate: float32 [1024, 4096], P(('dp', 'blk')), may hold values from -0.1875 to 0.1875
- w_down: float32 [4096, 1024], P(('dp', 'blk')), may hold values from -0.09375 to 0.09375
- s_qk: float32 [1024], replicated, may hold values from 1 to 2
- alpha_attn: float32 [1024], replicated, may hold values from 0.2 to 0.8
- s_up: float32 [4096], replicated, may hold values from 0.5 to 2
- s_gate: float32 [4096], replicated, may hold values from 0.5 to 2
- alpha_mlp: float32 [1024], replicated, may hold values from 0.2 to 0.8
- cotangent: bfloat16 [8, 512, 1024], P('dp', 'blk'), may hold values from -6 to 6
Outputs:
- hidden_out: bfloat16 [8, 512, 1024], P('dp', 'blk')
- tokens_grad: float32 [8, 512, 1024], P('dp', 'blk')
- g_query: float32 [1024, 1024], P(('dp', 'blk'))
- g_key: float32 [1024, 1024], P(('dp', 'blk'))
- g_value: float32 [1024, 1024], P(('dp', 'blk'))
- g_out: float32 [1024, 1024], P(('dp', 'blk'))
- g_up: float32 [1024, 4096], P(('dp', 'blk'))
- g_gate: float32 [1024, 4096], P(('dp', 'blk'))
- g_down: float32 [4096, 1024], P(('dp', 'blk'))
- g_sqk: float32 [1024], P(('dp', 'blk'))
- g_alpha_attn: float32 [1024], P(('dp', 'blk'))
- g_s_up: float32 [4096], P(('dp', 'blk'))
- g_s_gate: float32 [4096], P(('dp', 'blk'))
- g_alpha_mlp: float32 [1024], P(('dp', 'blk'))
Inputs may be any that keep to these rules, and one draw needn't show every extreme that they name: `doc_ids`: along each row the ids never fall, and every id from 0 to 7 occurs in every row.
All inputs are finite; a program needn't handle non-finite values.
Results may differ from a plain program's by a relative error of at most 0.03.
Values may be sent and summed in bfloat16 or wider, within the bound.
No kernel may reach another device: no remote copies, remote signals or barrier semaphores. Data moves between devices by JAX's collectives and lax.ppermute only.
A program may use at most 320 MiB of HBM per device.

v0:
```python
import math

import jax
import jax.numpy as jnp
from jax import lax
from jax.experimental import pallas as pl
from jax.experimental.pallas import tpu as pltpu
from jax.sharding import Mesh
from jax.sharding import PartitionSpec as P

HEADS = 16
HEAD_DIM = 64
EPS = 1e-06
NEG = -1e30
BF = jnp.bfloat16
F32 = jnp.float32


def dot(a, b):
    return jnp.dot(a, b, preferred_element_type=F32)


def dot_t(a, b):
    return lax.dot_general(a, b, (((1,), (1,)), ((), ())), preferred_element_type=F32)


def tdot(a, b):
    return lax.dot_general(a, b, (((0,), (0,)), ((), ())), preferred_element_type=F32)


def rotate(tensor, cosines, sines):
    half_dim = tensor.shape[-1] // 2
    front = tensor[..., :half_dim]
    behind = tensor[..., half_dim:]
    return jnp.concatenate(
        [front * cosines - behind * sines, behind * cosines + front * sines], axis=-1
    )


def sphere(tensor):
    return tensor * lax.rsqrt(jnp.mean(tensor * tensor, axis=-1, keepdims=True) + EPS)


def head_unit(tensor, gains):
    return gains * tensor * lax.rsqrt(jnp.sum(tensor * tensor, axis=-1, keepdims=True) + EPS)


def residual_step(branch, residual_in, alpha):
    return sphere(residual_in + alpha * (sphere(branch) - residual_in))


def gating(up_proj, gate_proj, scale_up, scale_gate):
    return scale_up * up_proj * jax.nn.silu(scale_gate * gate_proj)


def make_plain(sizes):
    ny, nx, nw, nz, nc = sizes
    ndev = ny * nx * nw * nz * nc
    line = ("w", "z")
    nline = nw * nz
    quad = ("x", "z")
    nquad = nx * nz

    def swap(value, axes, count, k):
        return lax.ppermute(value, axes, [(i, i ^ k) for i in range(count)])

    def gather_rel(value, axes, count):
        return [value] + [swap(value, axes, count, k) for k in range(1, count)]

    def exchange_rel(chunks, axes, count):
        return [chunks[0]] + [swap(chunks[k], axes, count, k) for k in range(1, count)]

    def sum_rel(chunks, axes, count, kind=BF):
        got = exchange_rel([c.astype(kind) for c in chunks], axes, count)
        total = chunks[0].astype(F32)
        for piece in got[1:]:
            total = total + piece.astype(F32)
        return total

    def double(value, stages):
        for axis, count, k in stages:
            value = jnp.concatenate([value, swap(value, axis, count, k)], axis=0)
        return value

    def halve(value, stages, kind=BF):
        for axis, count, k in stages[::-1]:
            half = value.shape[0] // 2
            other = swap(value[half:].astype(kind), axis, count, k)
            value = value[:half].astype(F32) + other.astype(F32)
        return value

    def bits(axis, count):
        return [(axis, count, 1 << b) for b in range(count.bit_length() - 1)]

    def ranks(order):
        count = dict(y=ny, x=nx, w=nw, z=nz, c=nc)
        shape = [count[axis] for axis in order]
        found = {}
        for i, axis in enumerate(order):
            shifted = jnp.arange(count[axis]) ^ lax.axis_index(axis)
            found[axis] = shifted.reshape((-1,) + (1,) * (len(order) - 1 - i))
        flat = jnp.zeros(shape, jnp.int32)
        return found, flat

    def reorder(order, target):
        found, flat = ranks(order)
        count = dict(y=ny, x=nx, w=nw, z=nz, c=nc)
        index = flat
        for axis in target:
            index = index * count[axis] + found[axis]
        return index.reshape(-1)

    def place(pieces, rank):
        stack = jnp.stack(pieces)
        order = rank ^ jnp.arange(len(pieces))
        return jnp.take(stack, order, axis=0)

    def pick(array, rank, count):
        return [lax.dynamic_index_in_dim(array, rank ^ k, 0, False) for k in range(count)]

    def body(
        tokens, doc_ids, w_query, w_key, w_value, w_out, w_up, w_gate, w_down,
        s_qk, alpha_attn, s_up, s_gate, alpha_mlp, cotangent,
    ):
        nseq, seg, dm = tokens.shape
        rows = w_query.shape[0]
        ff = w_up.shape[1]
        ffq = ff // nquad
        ffb = ff // ndev
        hcols = dm // nline
        nheads = HEADS // nline
        score_scale = math.sqrt(HEAD_DIM)
        c_at = lax.axis_index("c")
        line_at = lax.axis_index(line)
        quad_at = lax.axis_index(quad)

        def by_line(w):
            return w.astype(BF).reshape(rows, nline, hcols)

        w_qkv = jnp.stack([by_line(w_query), by_line(w_key), by_line(w_value)], axis=2)
        w_qkv = w_qkv.transpose(1, 0, 2, 3).reshape(nline, rows, 3 * hcols)
        got = jnp.stack(exchange_rel(pick(w_qkv, line_at, nline), line, nline))
        got = jnp.stack(gather_rel(got, ("y", "x"), ny * nx))
        full = double(got[None], bits("c", nc)).reshape(ndev, rows, 3 * hcols)
        full_qkv = jnp.take(full, reorder("yxwzc", "cyxwz"), axis=0).reshape(dm, 3 * hcols)
        full_out = lax.all_gather(w_out.astype(BF), ("y", "x", "w", "z", "c"), axis=0, tiled=True)

        def by_quad(w):
            w = w.astype(BF).reshape(rows, ny, nx, nw, nz, nc, ffb)
            return w.transpose(2, 4, 0, 1, 3, 5, 6).reshape(nquad, rows, ffq)

        w_ug = jnp.concatenate([by_quad(w_up), by_quad(w_gate)], axis=2)
        got = jnp.stack(exchange_rel(pick(w_ug, quad_at, nquad), quad, nquad))
        stages = bits("w", nw) + bits("y", ny) + bits("c", nc)

        def ff_full(part):
            full = double(part[None], stages).reshape(ndev, rows, ffq)
            return jnp.take(full, reorder("yxwzc", "cywxz"), axis=0).reshape(dm, ffq)

        full_up, full_gate = ff_full(got[:, :, :ffq]), ff_full(got[:, :, ffq:])
        full_down = double(w_down.astype(BF)[None], stages)
        full_down = jnp.take(full_down, reorder("ywc", "cyw"), axis=0).reshape(ffq, dm)

        def my_ff(vec):
            v = vec.reshape(ny, nx, nw, nz, nc, ffb).transpose(1, 3, 0, 2, 4, 5)
            return lax.dynamic_index_in_dim(v.reshape(nquad, ffq), quad_at, 0, False)

        my_s_up, my_s_gate = my_ff(s_up), my_ff(s_gate)
        my_gain = lax.dynamic_index_in_dim(s_qk.reshape(nline, hcols), line_at, 0, False)

        def to_row(value):
            keep = lax.dynamic_index_in_dim(value, c_at, 0, False)
            send = lax.dynamic_index_in_dim(value, 1 - c_at, 0, False)
            return jnp.concatenate([keep, lax.ppermute(send, "c", [(0, 1), (1, 0)])], axis=0)

        def from_row(value, send_type):
            keep, send = value[:seg], value[seg:]
            other = lax.ppermute(send.astype(send_type), "c", [(0, 1), (1, 0)])
            pair = jnp.stack([keep, other.astype(value.dtype)])
            return jnp.where(c_at == 0, pair, pair[::-1])

        docs = doc_ids.astype(BF)
        extra = jnp.zeros((nseq, 16, dm), BF).at[:, 0, :seg].set(docs)
        ext = jnp.concatenate([tokens, extra], axis=1)
        mine = to_row(ext).reshape(2, seg + 16, dm)
        everyone = jnp.stack(gather_rel(mine, line, nline))
        row_tokens = everyone[:, :, :seg].reshape(nline * 2 * seg, dm)
        row_docs = everyone[:, :, seg, :seg].reshape(-1).astype(F32)
        peers = line_at ^ jnp.arange(nline)
        seg_at = 2 * peers[:, None] + jnp.stack([c_at, 1 - c_at])[None, :]
        index = (seg_at[:, :, None] * seg + jnp.arange(seg)).reshape(-1)
        start = jnp.sum((row_docs[None, :] < row_docs[:, None]).astype(jnp.int32), axis=1)
        pos = index - start
        allowed = (index[None, :] <= index[:, None]) & (index[None, :] >= start[:, None])
        frequency = 10000.0 ** (-jnp.arange(HEAD_DIM // 2, dtype=F32) / (HEAD_DIM // 2))
        angles = pos.astype(F32)[:, None] * frequency
        cosines, sines = jnp.cos(angles)[:, None, :], jnp.sin(angles)[:, None, :]
        nt = row_tokens.shape[0]
        x_low = mine[:, :seg].reshape(2 * seg, dm)
        x_row = x_low.astype(F32)

        pre = dot(row_tokens, full_qkv)

        def heads(t):
            return t.reshape(nt, nheads, HEAD_DIM)

        def unit_pair(q_pre, k_pre, gains):
            gains = gains.reshape(nheads, HEAD_DIM)
            return (
                head_unit(rotate(heads(q_pre), cosines, sines), gains),
                head_unit(rotate(heads(k_pre), cosines, sines), gains),
            )

        (q_unit, k_unit), unit_pull = jax.vjp(
            unit_pair, pre[:, :hcols], pre[:, hcols : 2 * hcols], my_gain
        )
        q_low, k_low = q_unit.astype(BF), k_unit.astype(BF)
        v_low = heads(pre[:, 2 * hcols :].astype(BF))
        scores = jnp.einsum("qhd,khd->hqk", q_low, k_low, preferred_element_type=F32) * score_scale
        scores = jnp.where(allowed[None], scores, NEG)
        peak = jnp.max(scores, axis=-1, keepdims=True)
        raw = jnp.where(allowed[None], jnp.exp(scores - peak), 0.0)
        probs = raw / jnp.sum(raw, axis=-1, keepdims=True)
        p_low = probs.astype(BF)
        attended = jnp.einsum("hqk,khd->qhd", p_low, v_low, preferred_element_type=F32)
        att_low = attended.astype(BF).reshape(nline, 2 * seg, hcols)
        got = place(exchange_rel([att_low[k] for k in range(nline)], line, nline), line_at)
        att_mine = got.transpose(1, 0, 2).reshape(2 * seg, dm)

        h_attn = dot(att_mine, full_out)
        h_one, attn_pull = jax.vjp(residual_step, h_attn, x_row, alpha_attn)
        h_low = jnp.concatenate(gather_rel(h_one.astype(BF), quad, nquad), axis=0)
        up, gate = dot(h_low, full_up), dot(h_low, full_gate)
        mixed, gate_pull = jax.vjp(gating, up, gate, my_s_up, my_s_gate)
        mixed_low = mixed.astype(BF)
        part = dot(mixed_low, full_down).reshape(nquad, 2 * seg, dm)
        h_mlp = sum_rel([part[k] for k in range(nquad)], quad, nquad)
        result, out_pull = jax.vjp(residual_step, h_mlp, h_one, alpha_mlp)
        hidden_out = from_row(result.astype(BF), BF)

        d_result = to_row(cotangent).astype(F32)
        d_hmlp, d_hone, g_alpha_mlp = out_pull(d_result)
        dm_low = jnp.concatenate(gather_rel(d_hmlp.astype(BF), quad, nquad), axis=0)
        d_mixed = dot_t(dm_low, full_down)
        d_up, d_gate, g_s_up, g_s_gate = gate_pull(d_mixed)
        du_low, dg_low = d_up.astype(BF), d_gate.astype(BF)
        part = dot_t(du_low, full_up) + dot_t(dg_low, full_gate)
        part = part.reshape(nquad, 2 * seg, dm)
        d_hone = d_hone + sum_rel([part[k] for k in range(nquad)], quad, nquad)
        g_down = tdot(mixed_low, dm_low).reshape(ny * nw * nc, ffb, dm)
        g_down = halve(jnp.take(g_down, reorder("cyw", "ywc"), axis=0), stages)[0]

        def ff_scatter(left, right):
            part = tdot(left, right).reshape(ndev, rows, ffq)
            part = jnp.take(part, reorder("cywxz", "yxwzc"), axis=0)
            part = halve(part.reshape(ny * nw * nc, nquad, rows, ffq), stages)[0].astype(BF)
            got = place(exchange_rel([part[k] for k in range(nquad)], quad, nquad), quad_at)
            got = got.reshape(nx, nz, rows, ny, nw, nc, ffb).transpose(2, 3, 0, 4, 1, 5, 6)
            return got.reshape(rows, ff).astype(F32)

        g_up, g_gate = ff_scatter(h_low, du_low), ff_scatter(h_low, dg_low)

        d_hattn, d_tokens, g_alpha_attn = attn_pull(d_hone)
        dh_low = d_hattn.astype(BF)

        def to_owner(part, kind=BF):
            part = jnp.take(part, reorder("cyxwz", "yxwzc"), axis=0)
            part = halve(part.reshape((nc, ny * nx, nline) + part.shape[1:]), bits("c", nc), kind)[0]
            part = sum_rel([part[k] for k in range(ny * nx)], ("y", "x"), ny * nx, kind)
            return sum_rel([part[k] for k in range(nline)], line, nline, kind)

        g_out = to_owner(tdot(att_mine, dh_low).reshape(ndev, rows, dm))
        d_att = dot_t(dh_low, full_out).astype(BF).reshape(2 * seg, nline, hcols).transpose(1, 0, 2)
        d_att = jnp.concatenate(
            exchange_rel(pick(d_att, line_at, nline), line, nline), axis=0
        ).reshape(nt, nheads, HEAD_DIM)
        delta = jnp.sum(d_att.astype(F32) * attended, axis=-1)
        d_probs = jnp.einsum("qhd,khd->hqk", d_att, v_low, preferred_element_type=F32)
        d_scores = (probs * (d_probs - delta.T[:, :, None])).astype(BF)
        d_q = score_scale * jnp.einsum("hqk,khd->qhd", d_scores, k_low, preferred_element_type=F32)
        d_k = score_scale * jnp.einsum("hqk,qhd->khd", d_scores, q_low, preferred_element_type=F32)
        d_v = jnp.einsum("hqk,qhd->khd", p_low, d_att, preferred_element_type=F32)
        d_qpre, d_kpre, g_sqk = unit_pull((d_q, d_k))
        d_qkv = jnp.concatenate([d_qpre, d_kpre, d_v.reshape(nt, hcols)], axis=1).astype(BF)
        part = dot_t(d_qkv, full_qkv).reshape(nline, 2 * seg, dm)
        tokens_grad = d_tokens + sum_rel([part[k] for k in range(nline)], line, nline)
        tokens_grad = from_row(tokens_grad, BF)
        g_qkv = tdot(row_tokens, d_qkv).reshape(ndev, rows, 3 * hcols)
        g_qkv = jnp.take(g_qkv, reorder("cyxwz", "yxwzc"), axis=0)
        g_qkv = halve(g_qkv.reshape(nc, ny * nx, nline, rows, 3 * hcols), bits("c", nc))[0]
        g_qkv = sum_rel([g_qkv[k] for k in range(ny * nx)], ("y", "x"), ny * nx).astype(BF)
        got = place(exchange_rel([g_qkv[k] for k in range(nline)], line, nline), line_at)
        got = got.reshape(nline, rows, 3, hcols).transpose(2, 1, 0, 3).reshape(3, rows, dm)
        g_query, g_key, g_value = got.astype(F32)

        def spread(vec, rank, count):
            return jnp.where(jnp.arange(count)[:, None] == rank, vec[None], 0.0)

        def ff_order(vec):
            v = spread(vec, quad_at, nquad).reshape(nx, nz, ny, nw, nc, ffb)
            return v.transpose(2, 0, 3, 1, 4, 5).reshape(ndev, ffb)

        vecs = jnp.concatenate(
            [
                spread(g_sqk, line_at, nline).reshape(ndev, -1),
                g_alpha_attn.reshape(ndev, -1),
                ff_order(g_s_up),
                ff_order(g_s_gate),
                g_alpha_mlp.reshape(ndev, -1),
            ],
            axis=1,
        )
        vecs = to_owner(vecs, F32)
        cuts = [rows, 2 * rows, 2 * rows + ffb, 2 * rows + 2 * ffb]
        g_sqk, g_alpha_attn, g_s_up, g_s_gate, g_alpha_mlp = jnp.split(vecs, cuts)
        return (
            hidden_out, tokens_grad, g_query, g_key, g_value, g_out, g_up, g_gate, g_down,
            g_sqk, g_alpha_attn, g_s_up, g_s_gate, g_alpha_mlp,
        )

    return body


VM = pl.BlockSpec(memory_space=pltpu.VMEM)
SM = pl.BlockSpec(memory_space=pltpu.SMEM)
HB = pl.BlockSpec(memory_space=pltpu.HBM)


def call(kernel, outs, args, hbm=(), hbm_out=(), scratch=(), flops=0, mib=60, after=()):
    moved = sum(math.prod(a.shape) * a.dtype.itemsize for a in args)
    moved += sum(math.prod(s) * jnp.dtype(d).itemsize for s, d in outs)
    specs = [SM] + [HB if i in hbm else VM for i in range(1, len(args))]
    return pl.pallas_call(
        kernel,
        out_shape=[jax.ShapeDtypeStruct(s, d) for s, d in outs],
        in_specs=specs,
        out_specs=[HB if i in hbm_out else VM for i in range(len(outs))],
        scratch_shapes=list(scratch),
        compiler_params=pltpu.CompilerParams(vmem_limit_bytes=mib << 20),
        cost_estimate=pl.CostEstimate(flops=flops, bytes_accessed=moved, transcendentals=0),
    )(*args)


def row_norm(v):
    return lax.rsqrt(jnp.mean(v * v, axis=-1, keepdims=True) + EPS)


def sphere_back(dy, y, norm):
    return (dy - y * jnp.mean(dy * y, axis=-1, keepdims=True)) * norm


def make_kernels(sizes):
    ny, nx, nw, nz, nc = sizes
    ndev = ny * nx * nw * nz * nc
    nyx, nline = ny * nx, nw * nz
    nquad, nblk = nyx, nw * nz * nc
    line, yx = ("w", "z"), ("y", "x")
    quad, blk = yx, ("w", "z", "c")

    def swap(value, axes, count, k):
        return lax.ppermute(value, axes, [(i, i ^ k) for i in range(count)])

    def exchange(chunks, axes, count):
        return [chunks[0]] + [swap(chunks[k], axes, count, k) for k in range(1, count)]

    def gather(value, axes, count):
        return exchange([value] * count, axes, count)

    def body(
        tokens, doc_ids, w_query, w_key, w_value, w_out, w_up, w_gate, w_down,
        s_qk, alpha_attn, s_up, s_gate, alpha_mlp, cotangent,
    ):
        nseq, seg, dm = tokens.shape
        rows = w_query.shape[0]
        ff = w_up.shape[1]
        ffq, ffb = ff // nquad, ff // ndev
        hc = dm // nline
        nheads = HEADS // nline
        nt = nline * 2 * seg
        tk = 2 * seg
        pad = 16
        ext = seg + pad
        scale = math.sqrt(HEAD_DIM)
        tile = 256

        at = [lax.axis_index(a) for a in "yxwzc"]
        ranks = jnp.stack(at + [lax.axis_index(yx), lax.axis_index(line)])
        ranks = ranks.astype(jnp.int32)

        def pack_tokens(rk, tok, docs, keep, send):
            c = rk[4]
            first = lax.broadcasted_iota(jnp.int32, (pad, dm), 0) == 0
            for out, which in ((keep, c), (send, 1 - c)):
                out[:seg] = tok[which]
                out[seg:] = jnp.where(first, docs[which], 0.0).astype(BF)

        docs = jnp.pad(doc_ids.astype(F32), ((0, 0), (0, dm - seg))).reshape(nseq, 1, dm)
        keep, send = call(pack_tokens, [((ext, dm), BF)] * 2, (ranks, tokens, docs))
        mine = jnp.concatenate([keep, swap(send, "c", nc, 1)], axis=0)

        def pack_qkv(rk, wq, wk, wv, gain, *outs):
            for k in range(nline):
                cols = pl.ds(pl.multiple_of((rk[6] ^ k) * hc, 128), hc)
                for i, w in enumerate((wq, wk, wv)):
                    outs[k][:, i * hc : (i + 1) * hc] = w[:, cols].astype(BF)
            outs[nline][...] = gain[pl.ds(rk[6], 1), :]

        packed = call(
            pack_qkv,
            [((rows, 3 * hc), BF)] * nline + [((1, hc), F32)],
            (ranks, w_query, w_key, w_value, s_qk.reshape(nline, hc)),
        )
        qkv_parts, my_gain = packed[:nline], packed[nline]

        def pack_ff(rk, wu, wg, su, sg, *outs):
            for k in range(nquad):
                cols = pl.ds(pl.multiple_of((rk[5] ^ k) * ffq, 128), ffq)
                outs[k][:, :ffq] = wu[:, cols].astype(BF)
                outs[k][:, ffq:] = wg[:, cols].astype(BF)
            outs[nquad][...] = su[pl.ds(rk[5], 1), :]
            outs[nquad + 1][...] = sg[pl.ds(rk[5], 1), :]

        packed = call(
            pack_ff,
            [((rows, 2 * ffq), BF)] * nquad + [((1, ffq), F32)] * 2,
            (ranks, w_up, w_gate, s_up.reshape(nquad, ffq), s_gate.reshape(nquad, ffq)),
        )
        ug_parts, my_su, my_sg = packed[:nquad], *packed[nquad:]

        def pack_rest(rk, wo, wd, out_o, out_d):
            out_o[...] = wo[...].astype(BF)
            out_d[...] = wd[...].astype(BF)

        out_low, down_low = call(
            pack_rest, [((rows, dm), BF), ((ffb, dm), BF)], (ranks, w_out, w_down)
        )

        pieces = gather(mine, line, nline)
        got = jnp.stack(exchange(qkv_parts, line, nline))
        qkv_near = jnp.stack(gather(got, yx, nyx))
        qkv_far = swap(qkv_near, "c", nc, 1)
        got = jnp.stack(gather(out_low, line, nline))
        out_near = jnp.stack(gather(got, yx, nyx))
        out_far = swap(out_near, "c", nc, 1)
        got = jnp.concatenate(exchange(ug_parts, quad, nquad), axis=0)
        ug_full = lax.all_gather(got, blk, axis=0, tiled=True)
        down_near = down_low[None]
        for axis, count in (("w", nw), ("z", nz)):
            for b in range(count.bit_length() - 1):
                other = swap(down_near, axis, count, 1 << b)
                down_near = jnp.concatenate([down_near, other], axis=0)
        down_far = swap(down_near, "c", nc, 1)

        place = jnp.arange(nt, dtype=F32)[:, None]
        freq = 10000.0 ** (-jnp.arange(HEAD_DIM // 2, dtype=F32) / (HEAD_DIM // 2))
        angles = place * freq
        cosines, sines = jnp.cos(angles), jnp.sin(angles)
        reps = 128 // HEAD_DIM
        table = jnp.concatenate(
            [cosines] * (2 * reps) + [-sines, sines] * reps, axis=1
        )
        table_hi = table.astype(BF)
        table_lo = (table - table_hi.astype(F32)).astype(BF)

        def owner_copies(rk, near, far, dst, sems):
            copies = []
            for cr, src in enumerate((near, far)):
                for a in range(nyx):
                    for b in range(nline):
                        row = ((rk[5] ^ a) * nline + (rk[6] ^ b)) * nc + (rk[4] ^ cr)
                        row = pl.multiple_of(row * rows, 32)
                        copies.append(
                            pltpu.make_async_copy(
                                src.at[a, b], dst.at[pl.ds(row, rows)], sems.at[len(copies)]
                            )
                        )
            return copies

        def heads_swap(v, low):
            width = v.shape[1]
            half = HEAD_DIM // 2
            return jnp.where(low, pltpu.roll(v, width - half, 1), pltpu.roll(v, half, 1))

        def low_half():
            lane = lax.broadcasted_iota(jnp.int32, (nt, hc), 1)
            return lane % HEAD_DIM < HEAD_DIM // 2

        def token_index(rk, axis, shape):
            t = lax.broadcasted_iota(jnp.int32, shape, axis)
            peer = (t // tk) ^ rk[6]
            core = ((t // seg) % 2) ^ rk[4]
            return (peer * 2 + core) * seg + t % seg

        def allowed_keys(rk, start):
            key = token_index(rk, 1, (1, nt))
            query = token_index(rk, 0, (nt, 1))
            return (key <= query) & (key.astype(F32) >= start)

        def attn_forward(rk, *refs):
            ext_refs, refs = refs[:nline], refs[nline:]
            near, far, gain, t_hi, t_lo = refs[:5]
            att_outs, refs = refs[5 : 5 + nline], refs[5 + nline :]
            x_ref, w_ref, rq_ref, rk_ref, q_ref, k_ref, v_ref, start_ref, cs_ref, sems = refs
            copies = owner_copies(rk, near, far, w_ref, sems)
            for copy in copies:
                copy.start()
            ids = []
            for k in range(nline):
                for half in range(2):
                    block = ext_refs[k][half * ext : half * ext + seg, :]
                    x_ref[k * tk + half * seg : k * tk + (half + 1) * seg, :] = block
                    tail = ext_refs[k][half * ext + seg : (half + 1) * ext, :128].astype(F32)
                    ids.append(tail[:1, :seg])
            ids = jnp.concatenate(ids, axis=1)
            same = lax.broadcasted_iota(jnp.int32, (nt, nt), 0) == lax.broadcasted_iota(
                jnp.int32, (nt, nt), 1
            )
            ids_col = jnp.sum(jnp.where(same, ids, 0.0), axis=1, keepdims=True)
            start = jnp.sum(jnp.where(ids < ids_col, 1.0, 0.0), axis=1, keepdims=True)
            start_ref[...] = jnp.broadcast_to(start, (nt, 128))
            pos = token_index(rk, 0, (nt, 1)) - start.astype(jnp.int32)
            hot = (lax.broadcasted_iota(jnp.int32, (nt, nt), 1) == pos).astype(F32).astype(BF)
            cs = dot(hot, t_hi[...]) + dot(hot, t_lo[...])
            cs_ref[...] = cs
            cos = jnp.concatenate([cs[:, :128]] * (hc // 128), axis=1)
            sin = jnp.concatenate([cs[:, 128:]] * (hc // 128), axis=1)
            allowed = allowed_keys(rk, start)
            for copy in copies:
                copy.wait()
            low = low_half()
            for i, (raw_ref, unit_ref) in enumerate(((rq_ref, q_ref), (rk_ref, k_ref))):
                pre = dot(x_ref[...], w_ref[:, i * hc : (i + 1) * hc])
                turned = pre * cos + heads_swap(pre, low) * sin
                raw_ref[...] = turned
                for h in range(nheads):
                    at_h = slice(h * HEAD_DIM, (h + 1) * HEAD_DIM)
                    part = turned[:, at_h]
                    norm = lax.rsqrt(jnp.sum(part * part, axis=1, keepdims=True) + EPS)
                    unit_ref[:, at_h] = (gain[:, at_h] * part * norm).astype(BF)
            v_ref[...] = dot(x_ref[...], w_ref[:, 2 * hc :]).astype(BF)
            for h in range(nheads):
                at_h = slice(h * HEAD_DIM, (h + 1) * HEAD_DIM)
                s = dot_t(q_ref[:, at_h], k_ref[:, at_h]) * scale
                s = jnp.where(allowed, s, NEG)
                raw = jnp.exp(s - jnp.max(s, axis=1, keepdims=True))
                p = raw * (1.0 / jnp.sum(raw, axis=1, keepdims=True))
                att = dot(p.astype(BF), v_ref[:, at_h]).astype(BF)
                for k in range(nline):
                    att_outs[k][:, at_h] = att[k * tk : (k + 1) * tk]

        unit = ((nt, hc), BF)
        outs = call(
            attn_forward,
            [((tk, hc), BF)] * nline
            + [((nt, dm), BF), ((dm, 3 * hc), BF), ((nt, hc), F32), ((nt, hc), F32)]
            + [unit, unit, unit, ((nt, 128), F32), ((nt, 256), F32)],
            (ranks, *pieces, qkv_near, qkv_far, my_gain, table_hi, table_lo),
            hbm=(1 + nline, 2 + nline),
            scratch=[pltpu.SemaphoreType.DMA((ndev,))],
            flops=2 * nt * dm * 3 * hc + 4 * nt * nt * hc,
        )
        att_parts, outs = outs[:nline], outs[nline:]
        x_all, qkv_full, r_q, r_k, q_low, k_low, v_low, start, cs = outs
        att_got = exchange(att_parts, line, nline)

        def own_x(ext_ref):
            return jnp.concatenate([ext_ref[:seg], ext_ref[ext : ext + seg]], axis=0).astype(F32)

        def attn_update(rk, *refs):
            parts, refs = refs[:nline], refs[nline:]
            near, far, ext_ref, alpha, low_ref, one_ref, raw_ref, w, sems = refs
            copies = owner_copies(rk, near, far, w, sems)
            for copy in copies:
                copy.start()
            for copy in copies:
                copy.wait()
            total = None
            for k in range(nline):
                w_k = w[pl.ds(pl.multiple_of((rk[6] ^ k) * hc, hc), hc), :]
                term = dot(parts[k][...], w_k)
                total = term if total is None else total + term
            raw_ref[...] = total
            x = own_x(ext_ref)
            z = x + alpha[...] * (total * row_norm(total) - x)
            one = z * row_norm(z)
            one_ref[...] = one
            low_ref[...] = one.astype(BF)

        alpha_a, alpha_m = alpha_attn.reshape(1, dm), alpha_mlp.reshape(1, dm)
        full = ((tk, dm), F32)
        h_low, h_one, h_attn, full_out = call(
            attn_update,
            [((tk, dm), BF), full, full, ((dm, dm), BF)],
            (ranks, *att_got, out_near, out_far, mine, alpha_a),
            hbm=(1 + nline, 2 + nline),
            scratch=[pltpu.SemaphoreType.DMA((ndev,))],
            flops=2 * tk * dm * dm,
        )

        h_got = gather(h_low, quad, nquad)

        def load_ff(rk, stack, near, far, scratch):
            wug, wd, sems, sems_d = scratch
            first, second = [], []
            for b in range(nblk):
                for k in range(nquad):
                    row = pl.multiple_of(((rk[5] ^ k) * nblk + b) * rows, 32)
                    src = stack.at[pl.ds((b * nquad + k) * rows, rows)]
                    sem = sems.at[len(first)]
                    first.append(pltpu.make_async_copy(src, wug.at[pl.ds(row, rows)], sem))
            for cr, src in enumerate((near, far)):
                for a in range(nline):
                    peer = ((a % nw) * nz + a // nw) ^ rk[6]
                    row = pl.multiple_of((peer * nc + (rk[4] ^ cr)) * ffb, 32)
                    sem = sems_d.at[len(second)]
                    second.append(pltpu.make_async_copy(src.at[a], wd.at[pl.ds(row, ffb)], sem))
            return first, second

        w_scratch = [pltpu.VMEM((dm, 2 * ffq), BF), pltpu.VMEM((ffq, dm), BF)]
        w_scratch += [pltpu.SemaphoreType.DMA((ndev,)), pltpu.SemaphoreType.DMA((nblk,))]

        def gate_terms(gate, sg):
            v = sg * gate
            s = 1.0 / (1.0 + jnp.exp(-v))
            return v, s

        def ff_forward(rk, *refs):
            h_refs, stacks = refs[:nquad], refs[nquad : nquad + 3]
            su, sg = refs[nquad + 3 : nquad + 5]
            refs = refs[nquad + 5 :]
            parts, (h_all, up_ref, gate_ref, mixed_ref) = refs[:nquad], refs[nquad : nquad + 4]
            scratch = refs[nquad + 4 :]
            wug, wd = scratch[:2]
            first, third = load_ff(rk, *stacks, scratch)
            for copy in first + third:
                copy.start()
            for k in range(nquad):
                h_all[k * tk : (k + 1) * tk, :] = h_refs[k][...]
            for copy in first:
                copy.wait()

            @pl.loop(0, ffq // tile)
            def _(j):
                cols = pl.ds(pl.multiple_of(j * tile, tile), tile)
                up = dot(h_all[...], wug[:, cols])
                gate = dot(h_all[...], wug[:, pl.ds(pl.multiple_of(ffq + j * tile, tile), tile)])
                up_ref[:, cols] = up
                gate_ref[:, cols] = gate
                v, s = gate_terms(gate, sg[:, cols])
                mixed_ref[:, cols] = (su[:, cols] * up * (v * s)).astype(BF)

            for copy in third:
                copy.wait()

            @pl.loop(0, dm // tile)
            def _(j):
                cols = pl.ds(pl.multiple_of(j * tile, tile), tile)
                part = dot(mixed_ref[...], wd[:, cols])
                for k in range(nquad):
                    parts[k][:, cols] = part[k * tk : (k + 1) * tk].astype(parts[k].dtype)

        stacks = (ug_full, down_near, down_far)
        part_shapes = [((tk, dm), F32)] + [((tk, dm), BF)] * (nquad - 1)
        hbm = tuple(range(1 + nquad, 4 + nquad))
        outs = call(
            ff_forward,
            part_shapes + [((nt_q, dm), BF) for nt_q in (nquad * tk,)]
            + [((nquad * tk, ffq), F32)] * 2 + [((nquad * tk, ffq), BF)],
            (ranks, *h_got, *stacks, my_su, my_sg),
            hbm=hbm,
            scratch=w_scratch,
            flops=6 * nquad * tk * dm * ffq,
        )
        mlp_parts, (h_all, up, gate, mixed) = outs[:nquad], outs[nquad:]
        mlp_got = exchange(mlp_parts, quad, nquad)

        def split_rows(rk, cot, keep, send):
            keep[...] = cot[rk[4]]
            send[...] = cot[1 - rk[4]]

        half_low = ((seg, dm), BF)
        cot_keep, cot_send = call(split_rows, [half_low] * 2, (ranks, cotangent))
        cot_recv = swap(cot_send, "c", nc, 1)

        def mlp_update(rk, *refs):
            parts, refs = refs[:nquad], refs[nquad:]
            one_ref, alpha_ref, ck, cr, hid_keep, hid_send, dm_ref, direct, g_alpha = refs
            h = parts[0][...]
            for k in range(1, nquad):
                h = h + parts[k][...].astype(F32)
            one, alpha = one_ref[...], alpha_ref[...]
            norm_h = row_norm(h)
            b = h * norm_h
            gap = b - one
            z = one + alpha * gap
            norm_z = row_norm(z)
            y = z * norm_z
            low = y.astype(BF)
            hid_keep[...] = low[:seg]
            hid_send[...] = low[seg:]
            dy = jnp.concatenate([ck[...], cr[...]], axis=0).astype(F32)
            dz = sphere_back(dy, y, norm_z)
            g_alpha[...] = jnp.sum(dz * gap, axis=0, keepdims=True)
            direct[...] = dz * (1.0 - alpha)
            dm_ref[...] = sphere_back(dz * alpha, b, norm_h).astype(BF)

        outs = call(
            mlp_update,
            [half_low, half_low, ((tk, dm), BF), full, ((1, dm), F32)],
            (ranks, *mlp_got, h_one, alpha_m, cot_keep, cot_recv),
        )
        hid_keep, hid_send, dm_low, d_one_direct, g_alpha_mlp = outs
        hid_recv = swap(hid_send, "c", nc, 1)
        dm_got = gather(dm_low, quad, nquad)

        def ff_back(rk, *refs):
            d_refs, stacks = refs[:nquad], refs[nquad : nquad + 3]
            su_ref, sg_ref, up_ref, gate_ref = refs[nquad + 3 : nquad + 7]
            refs = refs[nquad + 7 :]
            parts, (d_all, dug, g_su, g_sg) = refs[:nquad], refs[nquad : nquad + 4]
            scratch = refs[nquad + 4 :]
            wug, wd = scratch[:2]
            first, third = load_ff(rk, *stacks, scratch)
            for copy in third + first:
                copy.start()
            for k in range(nquad):
                d_all[k * tk : (k + 1) * tk, :] = d_refs[k][...]
            for copy in third:
                copy.wait()

            @pl.loop(0, ffq // tile)
            def _(j):
                cols = pl.ds(pl.multiple_of(j * tile, tile), tile)
                d_mixed = dot_t(d_all[...], wd[cols, :])
                up, gate = up_ref[:, cols], gate_ref[:, cols]
                su, sg = su_ref[:, cols], sg_ref[:, cols]
                v, s = gate_terms(gate, sg)
                silu = v * s
                dug[:, cols] = (d_mixed * su * silu).astype(BF)
                slope = d_mixed * su * up * (s * (1.0 + v * (1.0 - s)))
                other = pl.ds(pl.multiple_of(ffq + j * tile, tile), tile)
                dug[:, other] = (slope * sg).astype(BF)
                g_su[:, cols] = jnp.sum(d_mixed * up * silu, axis=0, keepdims=True)
                g_sg[:, cols] = jnp.sum(slope * gate, axis=0, keepdims=True)

            for copy in first:
                copy.wait()

            @pl.loop(0, dm // tile)
            def _(j):
                cols = pl.ds(pl.multiple_of(j * tile, tile), tile)
                part = dot_t(dug[...], wug[cols, :])
                for k in range(nquad):
                    parts[k][:, cols] = part[k * tk : (k + 1) * tk].astype(parts[k].dtype)

        outs = call(
            ff_back,
            part_shapes + [((nquad * tk, dm), BF), ((nquad * tk, 2 * ffq), BF)] + [((1, ffq), F32)] * 2,
            (ranks, *dm_got, *stacks, my_su, my_sg, up, gate),
            hbm=hbm,
            scratch=w_scratch,
            flops=6 * nquad * tk * dm * ffq,
        )
        one_parts, (dm_all, dug_low, g_su, g_sg) = outs[:nquad], outs[nquad:]
        one_got = exchange(one_parts, quad, nquad)

        def store_blocks(scratch, outs, rows_of, count, depth, sems):
            copies = []
            for i, out in enumerate(outs):
                for r in range(count):
                    src = scratch.at[pl.ds(pl.multiple_of(rows_of(i, r) * depth, 32), depth)]
                    copies.append(pltpu.make_async_copy(src, out.at[r], sems.at[len(copies)]))
            return copies

        def down_row(rk, cr, r):
            peer = ((r % nw) * nz + r // nw) ^ rk[6]
            return peer * nc + (rk[4] ^ cr)

        def ff_row(rk, part, r):
            return (rk[5] ^ (r % nquad)) * nblk + r // nquad

        def own_row(rk, cr, r):
            return ((rk[5] ^ (r // nline)) * nline + (rk[6] ^ (r % nline))) * nc + (rk[4] ^ cr)

        def outer(row_of, count, depth, nout=2):
            def kernel(rk, left, right, *refs):
                outs, (g_ref, sems) = refs[:nout], refs[nout:]
                height = left.shape[1]

                @pl.loop(0, height // tile)
                def _(j):
                    cols = pl.ds(pl.multiple_of(j * tile, tile), tile)
                    g_ref[cols, :] = tdot(left[:, cols], right[...]).astype(BF)

                copies = store_blocks(
                    g_ref, outs, lambda i, r: row_of(rk, i, r), count, depth, sems
                )
                for copy in copies:
                    copy.start()
                for copy in copies:
                    copy.wait()

            def run(left, right):
                shape = ((count, depth, right.shape[1]), BF)
                return call(
                    kernel,
                    [shape] * nout,
                    (ranks, left, right),
                    hbm_out=tuple(range(nout)),
                    scratch=[
                        pltpu.VMEM((left.shape[1], right.shape[1]), BF),
                        pltpu.SemaphoreType.DMA((nout * count,)),
                    ],
                    flops=2 * left.shape[0] * left.shape[1] * right.shape[1],
                )

            return run

        def add(a, b):
            return a.astype(F32) + b.astype(F32)

        keep, send = outer(down_row, nline, ffb)(mixed, dm_all)
        total = add(keep, swap(send, "c", nc, 1))
        for axis, count in (("z", nz), ("w", nw)):
            for b in reversed(range(count.bit_length() - 1)):
                half = total.shape[0] // 2
                total = add(total[:half], swap(total[half:].astype(BF), axis, count, 1 << b))
        g_down = total[0]

        (g_ug,) = outer(ff_row, nblk * nquad, rows, 1)(h_all, dug_low)
        g_ug = g_ug.reshape(dm, 2 * ffq)
        g_ug = lax.psum_scatter(g_ug, blk, scatter_dimension=0, tiled=True)
        g_parts = exchange([g_ug[k * rows : (k + 1) * rows] for k in range(nquad)], quad, nquad)

        def place_ff(rk, *refs):
            parts, outs = refs[:nquad], refs[nquad:]
            for k in range(nquad):
                cols = pl.ds(pl.multiple_of((rk[5] ^ k) * ffq, 128), ffq)
                for i in range(2):
                    outs[i][:, cols] = parts[k][:, i * ffq : (i + 1) * ffq].astype(F32)

        g_up, g_gate = call(place_ff, [((rows, ff), F32)] * 2, (ranks, *g_parts))

        def attn_update_back(rk, *refs):
            parts, refs = refs[:nquad], refs[nquad:]
            direct_in, one_ref, raw_ref, ext_ref, alpha_ref, w = refs[:6]
            d_outs, (dh_ref, direct, g_alpha) = refs[6 : 6 + nline], refs[6 + nline :]
            d = direct_in[...] + parts[0][...]
            for k in range(1, nquad):
                d = d + parts[k][...].astype(F32)
            one, raw, alpha = one_ref[...], raw_ref[...], alpha_ref[...]
            x = own_x(ext_ref)
            norm_raw = row_norm(raw)
            b = raw * norm_raw
            gap = b - x
            norm_z = row_norm(x + alpha * gap)
            dz = sphere_back(d, one, norm_z)
            g_alpha[...] = jnp.sum(dz * gap, axis=0, keepdims=True)
            direct[...] = dz * (1.0 - alpha)
            dh_ref[...] = sphere_back(dz * alpha, b, norm_raw).astype(BF)
            for k in range(nline):
                w_k = w[pl.ds(pl.multiple_of((rk[6] ^ k) * hc, hc), hc), :]
                d_outs[k][...] = dot_t(dh_ref[...], w_k).astype(BF)

        outs = call(
            attn_update_back,
            [((tk, hc), BF)] * nline + [((tk, dm), BF), full, ((1, dm), F32)],
            (ranks, *one_got, d_one_direct, h_one, h_attn, mine, alpha_a, full_out),
            flops=2 * tk * dm * dm,
        )
        d_att_parts, (dh_low, d_x_direct, g_alpha_attn) = outs[:nline], outs[nline:]
        d_att = exchange(d_att_parts, line, nline)

        def attn_back(rk, *refs):
            d_refs, refs = refs[:nline], refs[nline:]
            w_ref, rq_ref, rk_ref, q_ref, k_ref, v_ref, start_ref, cs_ref, gain = refs[:9]
            parts, (d_ref, g_gain, do_ref, dq_ref, dk_ref) = refs[9 : 9 + nline], refs[9 + nline :]
            for k in range(nline):
                do_ref[k * tk : (k + 1) * tk, :] = d_refs[k][...]
            allowed = allowed_keys(rk, start_ref[:, :1])
            for h in range(nheads):
                at_h = slice(h * HEAD_DIM, (h + 1) * HEAD_DIM)
                q, key, do = q_ref[:, at_h], k_ref[:, at_h], do_ref[:, at_h]
                s = jnp.where(allowed, dot_t(q, key) * scale, NEG)
                raw = jnp.exp(s - jnp.max(s, axis=1, keepdims=True))
                p = raw * (1.0 / jnp.sum(raw, axis=1, keepdims=True))
                dp = dot_t(do, v_ref[:, at_h])
                pdp = p * dp
                delta = jnp.sum(pdp, axis=1, keepdims=True)
                ds = (pdp - p * delta).astype(BF)
                p = p.astype(BF)
                at_v = slice(2 * hc + h * HEAD_DIM, 2 * hc + (h + 1) * HEAD_DIM)
                d_ref[:, at_v] = tdot(p, do).astype(BF)
                dq_ref[:, at_h] = scale * dot(ds, key)
                dk_ref[:, at_h] = scale * tdot(ds, q)
            cs = cs_ref[...]
            cos = jnp.concatenate([cs[:, :128]] * (hc // 128), axis=1)
            sin = jnp.concatenate([cs[:, 128:]] * (hc // 128), axis=1)
            low = low_half()
            total = None
            for i, (raw_ref, g_ref) in enumerate(((rq_ref, dq_ref), (rk_ref, dk_ref))):
                for h in range(nheads):
                    at_h = slice(h * HEAD_DIM, (h + 1) * HEAD_DIM)
                    turned, g = raw_ref[:, at_h], g_ref[:, at_h]
                    norm = lax.rsqrt(jnp.sum(turned * turned, axis=1, keepdims=True) + EPS)
                    unit = turned * norm
                    term = jnp.sum(g * unit, axis=0, keepdims=True)
                    g_gain[:, at_h] = term if i == 0 else g_gain[:, at_h] + term
                    g = g * gain[:, at_h]
                    g_ref[:, at_h] = norm * (g - unit * jnp.sum(unit * g, axis=1, keepdims=True))
                g = g_ref[...]
                d_ref[:, i * hc : (i + 1) * hc] = (g * cos - heads_swap(g, low) * sin).astype(BF)

            @pl.loop(0, dm // tile)
            def _(j):
                cols = pl.ds(pl.multiple_of(j * tile, tile), tile)
                part = dot_t(d_ref[...], w_ref[cols, :])
                for k in range(nline):
                    parts[k][:, cols] = part[k * tk : (k + 1) * tk].astype(parts[k].dtype)

        outs = call(
            attn_back,
            [((tk, dm), F32)] + [((tk, dm), BF)] * (nline - 1)
            + [((nt, 3 * hc), BF), ((1, hc), F32)],
            (ranks, *d_att, qkv_full, r_q, r_k, q_low, k_low, v_low, start, cs, my_gain),
            scratch=[
                pltpu.VMEM((nt, hc), BF), pltpu.VMEM((nt, hc), F32), pltpu.VMEM((nt, hc), F32)
            ],
            flops=2 * nt * dm * 3 * hc + 10 * nt * nt * hc,
        )
        x_parts, (d_qkv, g_gain) = outs[:nline], outs[nline:]
        x_got = exchange(x_parts, line, nline)

        def finish_tokens(rk, *refs):
            parts, (direct, keep, send) = refs[:nline], refs[nline:]
            d = direct[...] + parts[0][...]
            for k in range(1, nline):
                d = d + parts[k][...].astype(F32)
            keep[...] = d[:seg]
            send[...] = d[seg:].astype(BF)

        x_keep, x_send = call(
            finish_tokens, [((seg, dm), F32), half_low], (ranks, *x_got, d_x_direct)
        )
        x_recv = swap(x_send, "c", nc, 1)

        def join_rows(rk, keep, recv, out):
            out[rk[4]] = keep[...].astype(out.dtype)
            out[1 - rk[4]] = recv[...].astype(out.dtype)

        (tokens_grad,) = call(join_rows, [((nseq, seg, dm), F32)], (ranks, x_keep, x_recv))
        (hidden_out,) = call(join_rows, [((nseq, seg, dm), BF)], (ranks, hid_keep, hid_recv))

        def sum_over(chunks, axes, count):
            got = exchange([chunks[0]] + [c.astype(BF) for c in chunks[1:]], axes, count)
            total = got[0].astype(F32)
            for piece in got[1:]:
                total = total + piece.astype(F32)
            return total

        def outer_out(rk, *refs):
            parts, (dh, keep, send, g_ref, sems) = refs[:nline], refs[nline:]
            for k in range(nline):
                spot = pl.ds(pl.multiple_of((rk[6] ^ k) * hc, hc), hc)
                g_ref[spot, :] = tdot(parts[k][...], dh[...]).astype(BF)
            copies = store_blocks(
                g_ref, (keep, send), lambda i, r: own_row(rk, i, r), nyx * nline, rows, sems
            )
            for copy in copies:
                copy.start()
            for copy in copies:
                copy.wait()

        shape = ((nyx * nline, rows, dm), BF)
        keep, send = call(
            outer_out,
            [shape, shape],
            (ranks, *att_got, dh_low),
            hbm_out=(0, 1),
            scratch=[pltpu.VMEM((dm, dm), BF), pltpu.SemaphoreType.DMA((2 * nyx * nline,))],
            flops=2 * tk * dm * dm,
        )

        def across(keep, send):
            total = add(keep, swap(send, "c", nc, 1))
            total = total.reshape((nyx, nline) + total.shape[1:])
            return sum_over([total[k] for k in range(nyx)], yx, nyx)

        total = across(keep, send)
        g_out = sum_over([total[k] for k in range(nline)], line, nline)
        total = across(*outer(own_row, nyx * nline, rows)(x_all, d_qkv)).astype(BF)
        got = exchange([total[k] for k in range(nline)], line, nline)

        def place_qkv(rk, *refs):
            parts, outs = refs[:nline], refs[nline:]
            for k in range(nline):
                cols = pl.ds(pl.multiple_of((rk[6] ^ k) * hc, 128), hc)
                for i in range(3):
                    outs[i][:, cols] = parts[k][:, i * hc : (i + 1) * hc].astype(F32)

        g_query, g_key, g_value = call(place_qkv, [((rows, dm), F32)] * 3, (ranks, *got))

        width = 2 * ffb + 3 * rows

        def spread(vec, rank, count):
            return jnp.where(jnp.arange(count)[:, None] == rank, vec[None], 0.0)

        def ff_order(vec):
            return spread(vec, ranks[5], nquad).reshape(ndev, ffb)

        at_line = ranks[6]
        vecs = jnp.concatenate(
            [
                spread(g_gain[0], at_line, nline).reshape(ndev, -1),
                g_alpha_attn.reshape(ndev, -1),
                ff_order(g_su[0]),
                ff_order(g_sg[0]),
                g_alpha_mlp.reshape(ndev, -1),
            ],
            axis=1,
        )
        order = (
            (jnp.arange(nc)[:, None, None] ^ at[4])
            + nc * (jnp.arange(nline)[None, None, :] ^ at_line)
            + nc * nline * (jnp.arange(nyx)[None, :, None] ^ ranks[5])
        ).reshape(-1)
        vecs = jnp.take(vecs, order, axis=0).reshape(nc, nyx, nline, width)
        vecs = vecs[0] + swap(vecs[1], "c", nc, 1)
        vecs = sum(exchange([vecs[k] for k in range(nyx)], yx, nyx))
        vecs = sum(exchange([vecs[k] for k in range(nline)], line, nline))
        cuts = [rows, 2 * rows, 2 * rows + ffb, 2 * rows + 2 * ffb]
        g_sqk, g_aa, g_s_up, g_s_gate, g_am = jnp.split(vecs, cuts)
        return (
            hidden_out, tokens_grad, g_query, g_key, g_value, g_out, g_up, g_gate, g_down,
            g_sqk, g_aa, g_s_up, g_s_gate, g_am,
        )

    return body


def make_body(sizes):
    plain, kernels = make_plain(sizes), make_kernels(sizes)
    ndev = math.prod(sizes)
    nline = sizes[2] * sizes[3]

    def body(*args):
        tokens, w_query, w_up = args[0], args[2], args[6]
        fits = w_query.shape[0] % 32 == 0 and (w_up.shape[1] // ndev) % 128 == 0
        fits = fits and (tokens.shape[2] // nline) % 256 == 0 and tokens.shape[1] == 64
        return (kernels if fits else plain)(*args)

    return body


def solution(mesh):
    ndp, nblk = mesh.shape["dp"], mesh.shape["blk"]
    sizes = (ndp // 2, 2, nblk // 4, 2, 2)
    fine = Mesh(mesh.devices.reshape(sizes), ("y", "x", "w", "z", "c"))
    rows, cols = ("y", "x"), ("w", "z", "c")
    flat = rows + cols
    seq = P(rows, cols, None)
    weight = P(flat, None)
    return jax.shard_map(
        make_body(sizes),
        mesh=fine,
        in_specs=(seq, P(rows, cols)) + (weight,) * 7 + (P(),) * 5 + (seq,),
        out_specs=(seq, seq) + (weight,) * 7 + (P(flat),) * 5,
        check_vma=False,
    )
```

profile of v0, /device:TPU:0, one launch (start us, length us, event | category | flops | bytes accessed | tf_op | source)
XLA Modules:
  0.0 401.9 jit_solution(10731414316370919909)
XLA Ops:
  19.7 3.8 collective-permute-done.25
  40.5 5.5 %collective-permute-done.15 = bf16[32,1024]{1,0:T(8,128)(2,1)S(1)} collective-permute-done((bf16[32,1024]{1,0:T(8,128)(2,1)}, bf16[32,1024]{1,0:T(8,128)(2,1)S(1)}, u32[]{:S(2)}, u32[]{:S(2)}) %collective-permute-start.15) | collective-permute-done | bytes 65568 | tf_op jit(solution)/shard_map/ppermute | solution.py:361
  50.6 25.7 %collective-permute-start.5 = (bf16[32,768]{1,0:T(8,128)(2,1)}, bf16[32,768]{1,0:T(8,128)(2,1)S(1)}, u32[]{:S(2)}, u32[]{:S(2)}) collective-permute-start(bf16[32,768]{1,0:T(8,128)(2,1)} %get-tuple-element.99), channel_id=1, source_target_pairs={{0,4},{2,6},{4,0},{6,2},{1,5},{3,7},{5,1},{7,3},{8,12},{10,14},{12... | collective-permute-start | bytes 147464 | tf_op jit(solution)/shard_map/ppermute | solution.py:361
  90.5 3.8 collective-permute-done.9
  99.1 4.6 %collective-permute-done.1.refs_1_ = bf16[160,1024]{1,0:T(8,128)(2,1)S(1)} collective-permute-done((bf16[160,1024]{1,0:T(8,128)(2,1)S(1)}, bf16[160,1024]{1,0:T(8,128)(2,1)S(1)}, u32[]{:S(2)}, u32[]{:S(2)}) %collective-permute-start.1) | collective-permute-done | bytes 327712 | tf_op jit(solution)/shard_map/ppermute | solution.py:361
  108.8 14.7 %collective-permute-done.2.refs_2_ = bf16[160,1024]{1,0:T(8,128)(2,1)} collective-permute-done((bf16[160,1024]{1,0:T(8,128)(2,1)S(1)}, bf16[160,1024]{1,0:T(8,128)(2,1)}, u32[]{:S(2)}, u32[]{:S(2)}) %collective-permute-start.2) | collective-permute-done | bytes 327712 | tf_op jit(solution)/shard_map/ppermute | solution.py:361
  123.5 10.8 %shard_map.256 = (bf16[128,256]{1,0:T(8,128)(2,1)}, bf16[128,256]{1,0:T(8,128)(2,1)}, bf16[128,256]{1,0:T(8,128)(2,1)}, bf16[128,256]{1,0:T(8,128)(2,1)}, bf16[5...) custom-call(s32[7]{0:T(128)} %stack.91.rk, ...), custom_call_target="tpu_custom_call" | custom-call | flops 1073741824 | bytes 8913948 | tf_op jit(solution)/shard_map/pallas_call | solution.py:333
  134.4 7.6 %collective-permute-start.11 = (bf16[128,256]{1,0:T(8,128)(2,1)}, bf16[128,256]{1,0:T(8,128)(2,1)S(1)}, u32[]{:S(2)}, u32[]{:S(2)}) collective-permute-start(bf16[128,256]{1,0:T(8,128)(2,1)} %get-tuple-element.103), channel_id=1, source_target_pairs={{0,2},{2,0},{4,6},{6,4},{1,3},{3,1},{5,7},{7,5},{8,10},{10,8},{12,... | collective-permute-start | bytes 196616 | tf_op jit(solution)/shard_map/ppermute | solution.py:361
  144.6 5.6 %collective-permute-done.12.refs_2_ = bf16[128,256]{1,0:T(8,128)(2,1)S(1)} collective-permute-done((bf16[128,256]{1,0:T(8,128)(2,1)}, bf16[128,256]{1,0:T(8,128)(2,1)S(1)}, u32[]{:S(2)}, u32[]{:S(2)}) %collective-permute-start.12) | collective-permute-done | bytes 65568 | tf_op jit(solution)/shard_map/ppermute | solution.py:361
  150.8 4.8 %shard_map.258 = (bf16[128,1024]{1,0:T(8,128)(2,1)}, f32[128,1024]{1,0:T(8,128)}, f32[128,1024]{1,0:T(8,128)}, bf16[1024,1024]{1,0:T(8,128)(2,1)}) custom-call(s32[7]{0:T(128)} %stack.91.rk, bf16[128,256]{1,0:T(8,128)(2,1)} %get-tuple-element.102.refs_0_, bf16[128,256]{1,0:T(8,128)(2,1)} %copy-done.22, bf16[128,256]{1,0:T(8,128)(2,1)} %copy-done.23, ...), custom_call_target="tpu_custom_call" | custom-call | flops 268435456 | bytes 6098972 | tf_op jit(solution)/shard_map/pallas_call | solution.py:333
  159.2 6.0 %collective-permute-done.21.refs_1_ = bf16[128,1024]{1,0:T(8,128)(2,1)S(1)} collective-permute-done((bf16[128,1024]{1,0:T(8,128)(2,1)}, bf16[128,1024]{1,0:T(8,128)(2,1)S(1)}, u32[]{:S(2)}, u32[]{:S(2)}) %collective-permute-start.21) | collective-permute-done | bytes 262176 | tf_op jit(solution)/shard_map/ppermute | solution.py:361
  165.2 4.4 %collective-permute-done.22.refs_2_ = bf16[128,1024]{1,0:T(8,128)(2,1)S(1)} collective-permute-done((bf16[128,1024]{1,0:T(8,128)(2,1)}, bf16[128,1024]{1,0:T(8,128)(2,1)S(1)}, u32[]{:S(2)}, u32[]{:S(2)}) %collective-permute-start.22) | collective-permute-done | bytes 262176 | tf_op jit(solution)/shard_map/ppermute | solution.py:361
  170.4 11.9 %shard_map.260 = (f32[128,1024]{1,0:T(8,128)}, bf16[128,1024]{1,0:T(8,128)(2,1)}, bf16[128,1024]{1,0:T(8,128)(2,1)}, bf16[128,1024]{1,0:T(8,128)(2,1)}, bf16[512...) custom-call(s32[7]{0:T(128)} %stack.91.rk, ...), custom_call_target="tpu_custom_call" | custom-call | flops 3221225472 | bytes 14950428 | tf_op jit(solution)/shard_map/pallas_call | solution.py:333
  190.4 4.1 %collective-permute-done.31.refs_2_ = bf16[128,1024]{1,0:T(8,128)(2,1)S(1)} collective-permute-done((bf16[128,1024]{1,0:T(8,128)(2,1)}, bf16[128,1024]{1,0:T(8,128)(2,1)S(1)}, u32[]{:S(2)}, u32[]{:S(2)}) %collective-permute-start.31) | collective-permute-done | bytes 262176 | tf_op jit(solution)/shard_map/ppermute | solution.py:361
  195.3 3.0 shard_map.262
  201.7 3.6 collective-permute-done.35.refs_1_
  205.4 4.1 %collective-permute-done.36.refs_2_ = bf16[128,1024]{1,0:T(8,128)(2,1)S(1)} collective-permute-done((bf16[128,1024]{1,0:T(8,128)(2,1)}, bf16[128,1024]{1,0:T(8,128)(2,1)S(1)}, u32[]{:S(2)}, u32[]{:S(2)}) %collective-permute-start.36) | collective-permute-done | bytes 262176 | tf_op jit(solution)/shard_map/ppermute | solution.py:361
  210.3 13.1 %shard_map.264 = (f32[128,1024]{1,0:T(8,128)}, bf16[128,1024]{1,0:T(8,128)(2,1)}, bf16[128,1024]{1,0:T(8,128)(2,1)}, bf16[128,1024]{1,0:T(8,128)(2,1)}, bf16[512...) custom-call(s32[7]{0:T(128)} %stack.91.rk, ...), custom_call_target="tpu_custom_call" | custom-call | flops 3221225472 | bytes 16007196 | tf_op jit(solution)/shard_map/pallas_call | solution.py:333
  223.4 7.4 %shard_map.272 = bf16[32,32,2048]{2,1,0:T(8,128)(2,1)} custom-call(s32[7]{0:T(128)} %stack.91.rk, bf16[512,1024]{1,0:T(8,128)(2,1)} %get-tuple-element.163.left, bf16[512,2048]{1,0:T(8,128)(2,1)} %get-tuple-element.164.right), custom_call_target="tpu_custom_call" | custom-call | flops 2147483648 | bytes 7340060 | tf_op jit(solution)/shard_map/pallas_call | solution.py:333
  242.4 4.8 %shard_map.265 = (bf16[128,256]{1,0:T(8,128)(2,1)}, bf16[128,256]{1,0:T(8,128)(2,1)}, bf16[128,256]{1,0:T(8,128)(2,1)}, bf16[128,256]{1,0:T(8,128)(2,1)}, bf16[1...) custom-call(s32[7]{0:T(128)} %stack.91.rk, f32[128,1024]{1,0:T(8,128)} %get-tuple-element.127.refs_0_, ...), custom_call_target="tpu_custom_call" | custom-call | flops 268435456 | bytes 6365212 | tf_op jit(solution)/shard_map/pallas_call | solution.py:333
  247.1 3.5 collective-permute-start.41
  255.7 5.6 %collective-permute-done.42.refs_2_ = bf16[128,256]{1,0:T(8,128)(2,1)S(1)} collective-permute-done((bf16[128,256]{1,0:T(8,128)(2,1)}, bf16[128,256]{1,0:T(8,128)(2,1)S(1)}, u32[]{:S(2)}, u32[]{:S(2)}) %collective-permute-start.42) | collective-permute-done | bytes 65568 | tf_op jit(solution)/shard_map/ppermute | solution.py:361
  262.5 13.7 %shard_map.266 = (f32[128,1024]{1,0:T(8,128)}, bf16[128,1024]{1,0:T(8,128)(2,1)}, bf16[128,1024]{1,0:T(8,128)(2,1)}, bf16[128,1024]{1,0:T(8,128)(2,1)}, bf16[512,768]{1,0:T(8,128)(2,1)}, /*index=5*/f32[1,256]{1,0:T(1,128)}) custom-call(s32[7]{0:T(128)} %stack.91.rk, bf16[128,256]{1,0:T(8,128)(2,1)} %get-tuple-element.134.refs_0_, ...), custom_call_target="tpu_custom_call" | custom-call | flops 1476395008 | bytes 6555676 | tf_op jit(solution)/shard_map/pallas_call | solution.py:333
  278.6 3.5 shard_map.271
  286.2 4.6 %shard_map.269 = (bf16[16,32,768]{2,1,0:T(8,128)(2,1)}, bf16[16,32,768]{2,1,0:T(8,128)(2,1)}) custom-call(s32[7]{0:T(128)} %stack.91.rk, bf16[512,1024]{1,0:T(8,128)(2,1)} %get-tuple-element.153.left, bf16[512,768]{1,0:T(8,128)(2,1)} %get-tuple-element.154.right), custom_call_target="tpu_custom_call" | custom-call | flops 805306368 | bytes 3407900 | tf_op jit(solution)/shard_map/pallas_call | solution.py:333
  296.4 5.0 %shard_map.274 = (bf16[4,128,1024]{2,1,0:T(8,128)(2,1)}, bf16[4,128,1024]{2,1,0:T(8,128)(2,1)}) custom-call(s32[7]{0:T(128)} %stack.91.rk, bf16[512,1024]{1,0:T(8,128)(2,1)} %get-tuple-element.167.left, bf16[512,1024]{1,0:T(8,128)(2,1)} %get-tuple-element.168.right), custom_call_target="tpu_custom_call" | custom-call | flops 1073741824 | bytes 4194332 | tf_op jit(solution)/shard_map/pallas_call | solution.py:333
  306.5 7.4 %collective-permute-done.44.refs_1_ = bf16[128,1024]{1,0:T(8,128)(2,1)S(1)} collective-permute-done((bf16[128,1024]{1,0:T(8,128)(2,1)S(1)}, bf16[128,1024]{1,0:T(8,128)(2,1)S(1)}, u32[]{:S(2)}, u32[]{:S(2)}) %collective-permute-start.44) | collective-permute-done | bytes 262176 | tf_op jit(solution)/shard_map/ppermute | solution.py:361
  313.9 10.2 %collective-permute-done.45.refs_2_ = bf16[128,1024]{1,0:T(8,128)(2,1)S(1)} collective-permute-done((bf16[128,1024]{1,0:T(8,128)(2,1)}, bf16[128,1024]{1,0:T(8,128)(2,1)S(1)}, u32[]{:S(2)}, u32[]{:S(2)}) %collective-permute-start.45) | collective-permute-done | bytes 262176 | tf_op jit(solution)/shard_map/ppermute | solution.py:361
  337.4 3.6 collective-permute-done.50
  344.4 4.5 %collective-permute-start.52 = (bf16[32,768]{1,0:T(8,128)(2,1)S(1)}, bf16[32,768]{1,0:T(8,128)(2,1)S(1)}, u32[]{:S(2)}, u32[]{:S(2)}) collective-permute-start(bf16[32,768]{1,0:T(8,128)(2,1)S(1)} %get-tuple-element.205), channel_id=1, source_target_pairs={{0,2},{2,0},{4,6},{6,4},{1,3},{3,1},{5,7},{7,5},{8,10},{10,8},{12,... | collective-permute-start | bytes 147464 | tf_op jit(solution)/shard_map/ppermute | solution.py:361
  358.9 6.7 %collective-permute-done.54.refs_3_ = bf16[32,768]{1,0:T(8,128)(2,1)S(1)} collective-permute-done((bf16[32,768]{1,0:T(8,128)(2,1)S(1)}, bf16[32,768]{1,0:T(8,128)(2,1)S(1)}, u32[]{:S(2)}, u32[]{:S(2)}) %collective-permute-start.54) | collective-permute-done | bytes 49184 | tf_op jit(solution)/shard_map/ppermute | solution.py:361
  374.3 7.6 %collective-permute-done.60 = bf16[32,1024]{1,0:T(8,128)(2,1)S(1)} collective-permute-done((bf16[32,1024]{1,0:T(8,128)(2,1)S(1)}, bf16[32,1024]{1,0:T(8,128)(2,1)S(1)}, u32[]{:S(2)}, u32[]{:S(2)}) %collective-permute-start.60) | collective-permute-done | bytes 65568 | tf_op jit(solution)/shard_map/ppermute | solution.py:361
  (316 shorter events, 161.9 us)
Async XLA Ops:
  7.2 162.4 %all-gather.2.cloned.1.call-start = ((), (), s32[]{:S(2)}) async-start(), calls=%async_computation.1 | async-start | bytes 4718592 | tf_op jit(solution)/shard_map/all_gather | solution.py:446
  25.3 357.3 %reduce-scatter.2.cloned.1.call-start = ((), (), s32[]{:S(2)}) async-start(), calls=%async_computation.2 | async-start | bytes 4718592 | tf_op jit(solution)/shard_map/reduce_scatter | solution.py:832
  27.2 12.7 %collective-permute-start.14 = (bf16[32,1024]{1,0:T(8,128)(2,1)}, bf16[32,1024]{1,0:T(8,128)(2,1)S(1)}, u32[]{:S(2)}, u32[]{:S(2)}) collective-permute-start(bf16[32,1024]{1,0:T(8,128)(2,1)} %get-tuple-element.106), channel_id=1, source_target_pairs={{0,2},{2,0},{4,6},{6,4},{1,3},{3,1},{5,7},{7,5},{8,10},{10,8},{12,... | collective-permute-start | bytes 196616 | tf_op jit(solution)/shard_map/ppermute | solution.py:361
  28.8 17.2 %collective-permute-start.15 = (bf16[32,1024]{1,0:T(8,128)(2,1)}, bf16[32,1024]{1,0:T(8,128)(2,1)S(1)}, u32[]{:S(2)}, u32[]{:S(2)}) collective-permute-start(bf16[32,1024]{1,0:T(8,128)(2,1)} %get-tuple-element.106), channel_id=1, source_target_pairs={{0,4},{2,6},{4,0},{6,2},{1,5},{3,7},{5,1},{7,3},{8,12},{10,14},{12... | collective-permute-start | bytes 196616 | tf_op jit(solution)/shard_map/ppermute | solution.py:361
  31.4 14.6 %collective-permute-start.16 = (bf16[32,1024]{1,0:T(8,128)(2,1)}, bf16[32,1024]{1,0:T(8,128)(2,1)S(1)}, u32[]{:S(2)}, u32[]{:S(2)}) collective-permute-start(bf16[32,1024]{1,0:T(8,128)(2,1)} %get-tuple-element.106), channel_id=1, source_target_pairs={{0,6},{2,4},{4,2},{6,0},{1,7},{3,5},{5,3},{7,1},{8,14},{10,12},{12... | collective-permute-start | bytes 196616 | tf_op jit(solution)/shard_map/ppermute | solution.py:361
  31.6 44.7 %collective-permute-start.27 = (bf16[1,128,1024]{2,1,0:T(8,128)(2,1)}, bf16[1,128,1024]{2,1,0:T(8,128)(2,1)S(1)}, u32[]{:S(2)}, u32[]{:S(2)}) collective-permute-start(bf16[1,128,1024]{2,1,0:T(8,128)(2,1)} %bitcast.78), channel_id=1, source_target_pairs={{0,4},{4,0},{1,5},{5,1},{2,6},{6,2},{3,7},{7,3},{8,12},{12,8},{9,1... | collective-permute-start | bytes 786440 | tf_op jit(solution)/shard_map/ppermute | solution.py:361
  35.7 14.9 %collective-permute-start.6 = (bf16[32,768]{1,0:T(8,128)(2,1)}, bf16[32,768]{1,0:T(8,128)(2,1)S(1)}, u32[]{:S(2)}, u32[]{:S(2)}) collective-permute-start(bf16[32,768]{1,0:T(8,128)(2,1)} %get-tuple-element.100), channel_id=1, source_target_pairs={{0,6},{2,4},{4,2},{6,0},{1,7},{3,5},{5,3},{7,1},{8,14},{10,12},{12... | collective-permute-start | bytes 147464 | tf_op jit(solution)/shard_map/ppermute | solution.py:361
  39.9 36.4 %collective-permute-start.4 = (bf16[32,768]{1,0:T(8,128)(2,1)}, bf16[32,768]{1,0:T(8,128)(2,1)S(1)}, u32[]{:S(2)}, u32[]{:S(2)}) collective-permute-start(bf16[32,768]{1,0:T(8,128)(2,1)} %get-tuple-element.98), channel_id=1, source_target_pairs={{0,2},{2,0},{4,6},{6,4},{1,3},{3,1},{5,7},{7,5},{8,10},{10,8},{12,... | collective-permute-start | bytes 147464 | tf_op jit(solution)/shard_map/ppermute | solution.py:361
  46.9 35.9 %collective-permute-start.17 = (bf16[4,32,1024]{2,1,0:T(8,128)(2,1)S(1)}, bf16[4,32,1024]{2,1,0:T(8,128)(2,1)S(1)}, u32[]{:S(2)}, u32[]{:S(2)}) collective-permute-start(bf16[4,32,1024]{2,1,0:T(8,128)(2,1)S(1)} %get-tuple-element.202), channel_id=1, source_target_pairs={{0,8},{8,0},{16,24},{24,16},{1,9},{9,1},{17,25},{25,17},{2,10},{10... | collective-permute-start | bytes 786440 | tf_op jit(solution)/shard_map/ppermute | solution.py:361
  48.5 34.8 %collective-permute-start.18 = (bf16[4,32,1024]{2,1,0:T(8,128)(2,1)S(1)}, bf16[4,32,1024]{2,1,0:T(8,128)(2,1)S(1)}, u32[]{:S(2)}, u32[]{:S(2)}) collective-permute-start(bf16[4,32,1024]{2,1,0:T(8,128)(2,1)S(1)} %get-tuple-element.202), channel_id=1, source_target_pairs={{0,16},{8,24},{16,0},{24,8},{1,17},{9,25},{17,1},{25,9},{2,18},{10... | collective-permute-start | bytes 786440 | tf_op jit(solution)/shard_map/ppermute | solution.py:361
  50.6 30.8 %collective-permute-start.5 = (bf16[32,768]{1,0:T(8,128)(2,1)}, bf16[32,768]{1,0:T(8,128)(2,1)S(1)}, u32[]{:S(2)}, u32[]{:S(2)}) collective-permute-start(bf16[32,768]{1,0:T(8,128)(2,1)} %get-tuple-element.99), channel_id=1, source_target_pairs={{0,4},{2,6},{4,0},{6,2},{1,5},{3,7},{5,1},{7,3},{8,12},{10,14},{12... | collective-permute-start | bytes 147464 | tf_op jit(solution)/shard_map/ppermute | solution.py:361
  81.4 15.8 %collective-permute-start.28 = (bf16[2,128,1024]{2,1,0:T(8,128)(2,1)S(1)}, bf16[2,128,1024]{2,1,0:T(8,128)(2,1)S(1)}, u32[]{:S(2)}, u32[]{:S(2)}) collective-permute-start(bf16[2,128,1024]{2,1,0:T(8,128)(2,1)S(1)} %pad_maximum_fusion.4), channel_id=1, source_target_pairs={{0,2},{2,0},{1,3},{3,1},{4,6},{6,4},{5,7},{7,5},{8,10},{10,8},{9,1... | collective-permute-start | bytes 1572872 | tf_op jit(solution)/shard_map/ppermute | solution.py:361
  86.4 17.2 %collective-permute-start.1 = (bf16[160,1024]{1,0:T(8,128)(2,1)S(1)}, bf16[160,1024]{1,0:T(8,128)(2,1)S(1)}, u32[]{:S(2)}, u32[]{:S(2)}) collective-permute-start(bf16[160,1024]{1,0:T(8,128)(2,1)S(1)} %constant_dynamic-update-slice_fusion.refs_0_.refs_6_.refs_7_), channel_id=1, source_target_pairs={{0,2},{2,0},{4,6},{6,4},{1,3},{3,1},{5,7},{7,5},{8,10},{10,8},{12,... | collective-permute-start | bytes 983048 | tf_op jit(solution)/shard_map/ppermute | solution.py:361
  89.8 60.4 %collective-permute-start.20 = (bf16[4,4,32,1024]{3,2,1,0:T(8,128)(2,1)S(1)}, bf16[4,4,32,1024]{3,2,1,0:T(8,128)(2,1)}, u32[]{:S(2)}, u32[]{:S(2)}) collective-permute-start(bf16[4,4,32,1024]{3,2,1,0:T(8,128)(2,1)S(1)} %pad_maximum_fusion.refs_4_), channel_id=1, source_target_pairs={{0,1},{1,0},{2,3},{3,2},{4,5},{5,4},{6,7},{7,6},{8,9},{9,8},{10,11... | collective-permute-start | bytes 3145736 | tf_op jit(solution)/shard_map/ppermute | solution.py:361
  94.5 29.0 %collective-permute-start.10 = (bf16[4,4,32,768]{3,2,1,0:T(8,128)(2,1)S(1)}, bf16[4,4,32,768]{3,2,1,0:T(8,128)(2,1)}, u32[]{:S(2)}, u32[]{:S(2)}) collective-permute-start(bf16[4,4,32,768]{3,2,1,0:T(8,128)(2,1)S(1)} %pad_maximum_fusion.2.refs_4_), channel_id=1, source_target_pairs={{0,1},{1,0},{2,3},{3,2},{4,5},{5,4},{6,7},{7,6},{8,9},{9,8},{10,11... | collective-permute-start | bytes 2359304 | tf_op jit(solution)/shard_map/ppermute | solution.py:361
  98.3 71.3 %collective-permute-start.29 = (bf16[4,128,1024]{2,1,0:T(8,128)(2,1)}, bf16[4,128,1024]{2,1,0:T(8,128)(2,1)}, u32[]{:S(2)}, u32[]{:S(2)}) collective-permute-start(bf16[4,128,1024]{2,1,0:T(8,128)(2,1)} %pad_maximum_fusion.1.refs_5_), channel_id=1, source_target_pairs={{0,1},{1,0},{2,3},{3,2},{4,5},{5,4},{6,7},{7,6},{8,9},{9,8},{10,11... | collective-permute-start | bytes 3145736 | tf_op jit(solution)/shard_map/ppermute | solution.py:361
  98.3 25.2 %collective-permute-start.2 = (bf16[160,1024]{1,0:T(8,128)(2,1)S(1)}, bf16[160,1024]{1,0:T(8,128)(2,1)}, u32[]{:S(2)}, u32[]{:S(2)}) collective-permute-start(bf16[160,1024]{1,0:T(8,128)(2,1)S(1)} %constant_dynamic-update-slice_fusion.refs_0_.refs_6_.refs_7_), channel_id=1, source_target_pairs={{0,4},{2,6},{4,0},{6,2},{1,5},{3,7},{5,1},{7,3},{8,12},{10,14},{12... | collective-permute-start | bytes 983048 | tf_op jit(solution)/shard_map/ppermute | solution.py:361
  103.6 19.9 %collective-permute-start.3 = (bf16[160,1024]{1,0:T(8,128)(2,1)S(1)}, bf16[160,1024]{1,0:T(8,128)(2,1)}, u32[]{:S(2)}, u32[]{:S(2)}) collective-permute-start(bf16[160,1024]{1,0:T(8,128)(2,1)S(1)} %constant_dynamic-update-slice_fusion.refs_0_.refs_6_.refs_7_), channel_id=1, source_target_pairs={{0,6},{2,4},{4,2},{6,0},{1,7},{3,5},{5,3},{7,1},{8,14},{10,12},{12... | collective-permute-start | bytes 983048 | tf_op jit(solution)/shard_map/ppermute | solution.py:361
  157.0 12.6 %collective-permute-start.22 = (bf16[128,1024]{1,0:T(8,128)(2,1)}, bf16[128,1024]{1,0:T(8,128)(2,1)S(1)}, u32[]{:S(2)}, u32[]{:S(2)}) collective-permute-start(bf16[128,1024]{1,0:T(8,128)(2,1)} %get-tuple-element.107.refs_0_), channel_id=1, source_target_pairs={{0,16},{8,24},{16,0},{24,8},{1,17},{9,25},{17,1},{25,9},{2,18},{10... | collective-permute-start | bytes 786440 | tf_op jit(solution)/shard_map/ppermute | solution.py:361
  282.1 48.7 %collective-permute-start.55 = (bf16[16,32,1024]{2,1,0:T(8,128)(2,1)}, bf16[16,32,1024]{2,1,0:T(8,128)(2,1)S(1)}, u32[]{:S(2)}, u32[]{:S(2)}) collective-permute-start(bf16[16,32,1024]{2,1,0:T(8,128)(2,1)} %get-tuple-element.162), channel_id=1, source_target_pairs={{0,1},{1,0},{2,3},{3,2},{4,5},{5,4},{6,7},{7,6},{8,9},{9,8},{10,11... | collective-permute-start | bytes 3145736 | tf_op jit(solution)/shard_map/ppermute | solution.py:361
  290.9 36.3 %collective-permute-start.48 = (bf16[16,32,768]{2,1,0:T(8,128)(2,1)}, bf16[16,32,768]{2,1,0:T(8,128)(2,1)}, u32[]{:S(2)}, u32[]{:S(2)}) collective-permute-start(bf16[16,32,768]{2,1,0:T(8,128)(2,1)} %get-tuple-element.156), channel_id=1, source_target_pairs={{0,1},{1,0},{2,3},{3,2},{4,5},{5,4},{6,7},{7,6},{8,9},{9,8},{10,11... | collective-permute-start | bytes 2359304 | tf_op jit(solution)/shard_map/ppermute | solution.py:361
  301.4 12.5 %collective-permute-start.44 = (bf16[128,1024]{1,0:T(8,128)(2,1)S(1)}, bf16[128,1024]{1,0:T(8,128)(2,1)S(1)}, u32[]{:S(2)}, u32[]{:S(2)}) collective-permute-start(bf16[128,1024]{1,0:T(8,128)(2,1)S(1)} %copy-done.35), channel_id=1, source_target_pairs={{0,2},{2,0},{4,6},{6,4},{1,3},{3,1},{5,7},{7,5},{8,10},{10,8},{12,... | collective-permute-start | bytes 786440 | tf_op jit(solution)/shard_map/ppermute | solution.py:361
  302.6 21.6 %collective-permute-start.45 = (bf16[128,1024]{1,0:T(8,128)(2,1)}, bf16[128,1024]{1,0:T(8,128)(2,1)S(1)}, u32[]{:S(2)}, u32[]{:S(2)}) collective-permute-start(bf16[128,1024]{1,0:T(8,128)(2,1)} %get-tuple-element.148), channel_id=1, source_target_pairs={{0,4},{2,6},{4,0},{6,2},{1,5},{3,7},{5,1},{7,3},{8,12},{10,14},{12... | collective-permute-start | bytes 786440 | tf_op jit(solution)/shard_map/ppermute | solution.py:361
  303.8 20.3 %collective-permute-start.46 = (bf16[128,1024]{1,0:T(8,128)(2,1)}, bf16[128,1024]{1,0:T(8,128)(2,1)S(1)}, u32[]{:S(2)}, u32[]{:S(2)}) collective-permute-start(bf16[128,1024]{1,0:T(8,128)(2,1)} %get-tuple-element.149), channel_id=1, source_target_pairs={{0,6},{2,4},{4,2},{6,0},{1,7},{3,5},{5,3},{7,1},{8,14},{10,12},{12... | collective-permute-start | bytes 786440 | tf_op jit(solution)/shard_map/ppermute | solution.py:361
  313.9 35.0 %collective-permute-start.65 = (bf16[4,128,1024]{2,1,0:T(8,128)(2,1)}, bf16[4,128,1024]{2,1,0:T(8,128)(2,1)S(1)}, u32[]{:S(2)}, u32[]{:S(2)}) collective-permute-start(bf16[4,128,1024]{2,1,0:T(8,128)(2,1)} %get-tuple-element.170), channel_id=1, source_target_pairs={{0,1},{1,0},{2,3},{3,2},{4,5},{5,4},{6,7},{7,6},{8,9},{9,8},{10,11... | collective-permute-start | bytes 3145736 | tf_op jit(solution)/shard_map/ppermute | solution.py:361
  327.2 17.3 %collective-permute-start.47 = (bf16[64,1024]{1,0:T(8,128)(2,1)}, bf16[64,1024]{1,0:T(8,128)(2,1)S(1)}, u32[]{:S(2)}, u32[]{:S(2)}) collective-permute-start(bf16[64,1024]{1,0:T(8,128)(2,1)} %get-tuple-element.152), channel_id=1, source_target_pairs={{0,1},{1,0},{2,3},{3,2},{4,5},{5,4},{6,7},{7,6},{8,9},{9,8},{10,11... | collective-permute-start | bytes 393224 | tf_op jit(solution)/shard_map/ppermute | solution.py:361
  336.5 31.3 %collective-permute-start.56 = (bf16[4,32,1024]{2,1,0:T(8,128)(2,1)}, bf16[4,32,1024]{2,1,0:T(8,128)(2,1)}, u32[]{:S(2)}, u32[]{:S(2)}) collective-permute-start(bf16[4,32,1024]{2,1,0:T(8,128)(2,1)} %get-tuple-element.188), channel_id=1, source_target_pairs={{0,8},{8,0},{16,24},{24,16},{1,9},{9,1},{17,25},{25,17},{2,10},{10... | collective-permute-start | bytes 786440 | tf_op jit(solution)/shard_map/ppermute | solution.py:361
  341.0 26.8 %collective-permute-start.57 = (bf16[4,32,1024]{2,1,0:T(8,128)(2,1)}, bf16[4,32,1024]{2,1,0:T(8,128)(2,1)}, u32[]{:S(2)}, u32[]{:S(2)}) collective-permute-start(bf16[4,32,1024]{2,1,0:T(8,128)(2,1)} %get-tuple-element.190), channel_id=1, source_target_pairs={{0,16},{8,24},{16,0},{24,8},{1,17},{9,25},{17,1},{25,9},{2,18},{10... | collective-permute-start | bytes 786440 | tf_op jit(solution)/shard_map/ppermute | solution.py:361
  341.9 25.9 %collective-permute-start.58 = (bf16[4,32,1024]{2,1,0:T(8,128)(2,1)S(1)}, bf16[4,32,1024]{2,1,0:T(8,128)(2,1)}, u32[]{:S(2)}, u32[]{:S(2)}) collective-permute-start(bf16[4,32,1024]{2,1,0:T(8,128)(2,1)S(1)} %get-tuple-element.189), channel_id=1, source_target_pairs={{0,24},{8,16},{16,8},{24,0},{1,25},{9,17},{17,9},{25,1},{2,26},{10... | collective-permute-start | bytes 786440 | tf_op jit(solution)/shard_map/ppermute | solution.py:361
  351.8 22.0 %collective-permute-start.66 = (bf16[2,128,1024]{2,1,0:T(8,128)(2,1)S(1)}, bf16[2,128,1024]{2,1,0:T(8,128)(2,1)S(1)}, u32[]{:S(2)}, u32[]{:S(2)}) collective-permute-start(bf16[2,128,1024]{2,1,0:T(8,128)(2,1)S(1)} %slice.239), channel_id=1, source_target_pairs={{0,2},{2,0},{1,3},{3,1},{4,6},{6,4},{5,7},{7,5},{8,10},{10,8},{9,1... | collective-permute-start | bytes 1572872 | tf_op jit(solution)/shard_map/ppermute | solution.py:361
  369.4 12.5 %collective-permute-start.60 = (bf16[32,1024]{1,0:T(8,128)(2,1)S(1)}, bf16[32,1024]{1,0:T(8,128)(2,1)S(1)}, u32[]{:S(2)}, u32[]{:S(2)}) collective-permute-start(bf16[32,1024]{1,0:T(8,128)(2,1)S(1)} %get-tuple-element.200), channel_id=1, source_target_pairs={{0,4},{2,6},{4,0},{6,2},{1,5},{3,7},{5,1},{7,3},{8,12},{10,14},{12... | collective-permute-start | bytes 196616 | tf_op jit(solution)/shard_map/ppermute | solution.py:361
  374.0 13.9 %collective-permute-start.67 = (bf16[1,128,1024]{2,1,0:T(8,128)(2,1)S(1)}, bf16[1,128,1024]{2,1,0:T(8,128)(2,1)S(1)}, u32[]{:S(2)}, u32[]{:S(2)}) collective-permute-start(bf16[1,128,1024]{2,1,0:T(8,128)(2,1)S(1)} %slice.240), channel_id=1, source_target_pairs={{0,4},{4,0},{1,5},{5,1},{2,6},{6,2},{3,7},{7,3},{8,12},{12,8},{9,1... | collective-permute-start | bytes 786440 | tf_op jit(solution)/shard_map/ppermute | solution.py:361
  (94 other events, 707.6 us)
Sparse Core Ops, SparseCore 0:
  25.4 62.0 all-gather.1
  231.0 54.5 reduce-scatter.1
where the time goes:
time: 403 us; the launch traced here: 402 us
  waiting for transfers between devices  129 us (32%)
  starting transfers between devices  118 us (29%)
  Pallas kernels  101 us (25%)
  local copies, waits for them, and re-layouts  20.7 us (5%)
  other arithmetic  17.5 us (4%)
  between operations  14.8 us (4%)
    ppermute x75, waiting for transfers between devices, swap(): return lax.ppermute(value, axes, [(i, i ^ k) for i in range(count)])  129 us
    ppermute x75, starting transfers between devices, swap(): return lax.ppermute(value, axes, [(i, i ^ k) for i in range(count)])  118 us
    pallas_call x21, Pallas kernels, call(): pl.pallas_call(kernel, out_shape=[jax.ShapeDtypeStruct(s, d) for s, d in...  101 us
    unnamed x99, local copies, waits for them, and re-layouts  8.66 us
  transfers between devices with their start and end apart: 77, of which 36 were waited for; matrix products, arithmetic and copies ran while one was open for 6% of the time, Pallas kernels for 15%

commit v1 on v0

--- a/solution.py
+++ b/solution.py
@@ -329,16 +329,22 @@
 def call(kernel, outs, args, hbm=(), hbm_out=(), scratch=(), flops=0, mib=60, after=()):
     moved = sum(math.prod(a.shape) * a.dtype.itemsize for a in args)
     moved += sum(math.prod(s) * jnp.dtype(d).itemsize for s, d in outs)
-    specs = [SM] + [HB if i in hbm else VM for i in range(1, len(args))]
+    count = len(args)
+
+    def run(*refs):
+        kernel(*refs[:count], *refs[count + len(after) :])
+
+    specs = [SM] + [HB if i in hbm else VM for i in range(1, count)]
+    specs += [pl.BlockSpec(memory_space=pl.ANY)] * len(after)
     return pl.pallas_call(
-        kernel,
+        run,
         out_shape=[jax.ShapeDtypeStruct(s, d) for s, d in outs],
         in_specs=specs,
         out_specs=[HB if i in hbm_out else VM for i in range(len(outs))],
         scratch_shapes=list(scratch),
         compiler_params=pltpu.CompilerParams(vmem_limit_bytes=mib << 20),
         cost_estimate=pl.CostEstimate(flops=flops, bytes_accessed=moved, transcendentals=0),
-    )(*args)
+    )(*args, *after)
 
 
 def row_norm(v):
@@ -353,9 +359,8 @@
     ny, nx, nw, nz, nc = sizes
     ndev = ny * nx * nw * nz * nc
     nyx, nline = ny * nx, nw * nz
-    nquad, nblk = nyx, nw * nz * nc
-    line, yx = ("w", "z"), ("y", "x")
-    quad, blk = yx, ("w", "z", "c")
+    ndpc = nyx * nc
+    line, yx, dpc = ("w", "z"), ("y", "x"), ("y", "x", "c")
 
     def swap(value, axes, count, k):
         return lax.ppermute(value, axes, [(i, i ^ k) for i in range(count)])
@@ -373,7 +378,8 @@
         nseq, seg, dm = tokens.shape
         rows = w_query.shape[0]
         ff = w_up.shape[1]
-        ffq, ffb = ff // nquad, ff // ndev
+        ffq, ffb = ff // nline, ff // ndev
+        sub = nc * ffb
         hc = dm // nline
         nheads = HEADS // nline
         nt = nline * 2 * seg
@@ -394,62 +400,69 @@
                 out[:seg] = tok[which]
                 out[seg:] = jnp.where(first, docs[which], 0.0).astype(BF)
 
+        def ff_cols(rk, k):
+            runs = [(d * nline + (rk[6] ^ k)) * sub for d in range(nyx)]
+            return [pl.ds(pl.multiple_of(run, 128), sub) for run in runs]
+
+        def pack_weights(rk, wq, wk, wv, wu, wg, wo, gain, su, sg, *outs):
+            for k in range(nline):
+                out, out_ff = outs[k], outs[nline + k]
+                cols = pl.ds(pl.multiple_of((rk[6] ^ k) * hc, 128), hc)
+                for i, w in enumerate((wq, wk, wv)):
+                    out[:, i * hc : (i + 1) * hc] = w[:, cols].astype(BF)
+                for d, cols in enumerate(ff_cols(rk, k)):
+                    for i, w in enumerate((wu, wg)):
+                        here = i * ffq + d * sub
+                        out_ff[:, here : here + sub] = w[:, cols].astype(BF)
+                out_ff[:, 2 * ffq :] = wo[...].astype(BF)
+            outs = outs[nline:]
+            outs[nline][...] = gain[:, pl.ds(pl.multiple_of(rk[6] * hc, 128), hc)]
+            for d, cols in enumerate(ff_cols(rk, 0)):
+                here = slice(d * sub, (d + 1) * sub)
+                outs[nline + 1][:, here] = su[:, cols]
+                outs[nline + 2][:, here] = sg[:, cols]
+
         docs = jnp.pad(doc_ids.astype(F32), ((0, 0), (0, dm - seg))).reshape(nseq, 1, dm)
         keep, send = call(pack_tokens, [((ext, dm), BF)] * 2, (ranks, tokens, docs))
         mine = jnp.concatenate([keep, swap(send, "c", nc, 1)], axis=0)
-
-        def pack_qkv(rk, wq, wk, wv, gain, *outs):
+        packed = call(
+            pack_weights,
+            [((rows, 3 * hc), BF)] * nline
+            + [((rows, 2 * ffq + dm), BF)] * nline
+            + [((1, hc), F32)]
+            + [((1, ffq), F32)] * 2,
+            (ranks, w_query, w_key, w_value, w_up, w_gate, w_out, s_qk.reshape(1, dm))
+            + (s_up.reshape(1, ff), s_gate.reshape(1, ff)),
+            after=(keep,),
+        )
+        packed, packed_ff, (my_gain, my_su, my_sg) = (
+            packed[:nline], packed[nline : 2 * nline], packed[2 * nline :]
+        )
+
+        w_got = exchange(packed, line, nline)
+        ff_got = exchange(packed_ff, line, nline)
+        pieces = gather(mine, line, nline)
+
+        def stack(rk, *refs):
             for k in range(nline):
-                cols = pl.ds(pl.multiple_of((rk[6] ^ k) * hc, 128), hc)
-                for i, w in enumerate((wq, wk, wv)):
-                    outs[k][:, i * hc : (i + 1) * hc] = w[:, cols].astype(BF)
-            outs[nline][...] = gain[pl.ds(rk[6], 1), :]
-
-        packed = call(
-            pack_qkv,
-            [((rows, 3 * hc), BF)] * nline + [((1, hc), F32)],
-            (ranks, w_query, w_key, w_value, s_qk.reshape(nline, hc)),
-        )
-        qkv_parts, my_gain = packed[:nline], packed[nline]
-
-        def pack_ff(rk, wu, wg, su, sg, *outs):
-            for k in range(nquad):
-                cols = pl.ds(pl.multiple_of((rk[5] ^ k) * ffq, 128), ffq)
-                outs[k][:, :ffq] = wu[:, cols].astype(BF)
-                outs[k][:, ffq:] = wg[:, cols].astype(BF)
-            outs[nquad][...] = su[pl.ds(rk[5], 1), :]
-            outs[nquad + 1][...] = sg[pl.ds(rk[5], 1), :]
-
-        packed = call(
-            pack_ff,
-            [((rows, 2 * ffq), BF)] * nquad + [((1, ffq), F32)] * 2,
-            (ranks, w_up, w_gate, s_up.reshape(nquad, ffq), s_gate.reshape(nquad, ffq)),
-        )
-        ug_parts, my_su, my_sg = packed[:nquad], *packed[nquad:]
-
-        def pack_rest(rk, wo, wd, out_o, out_d):
-            out_o[...] = wo[...].astype(BF)
-            out_d[...] = wd[...].astype(BF)
-
-        out_low, down_low = call(
-            pack_rest, [((rows, dm), BF), ((ffb, dm), BF)], (ranks, w_out, w_down)
-        )
-
-        pieces = gather(mine, line, nline)
-        got = jnp.stack(exchange(qkv_parts, line, nline))
-        qkv_near = jnp.stack(gather(got, yx, nyx))
-        qkv_far = swap(qkv_near, "c", nc, 1)
-        got = jnp.stack(gather(out_low, line, nline))
-        out_near = jnp.stack(gather(got, yx, nyx))
-        out_far = swap(out_near, "c", nc, 1)
-        got = jnp.concatenate(exchange(ug_parts, quad, nquad), axis=0)
-        ug_full = lax.all_gather(got, blk, axis=0, tiled=True)
-        down_near = down_low[None]
-        for axis, count in (("w", nw), ("z", nz)):
-            for b in range(count.bit_length() - 1):
-                other = swap(down_near, axis, count, 1 << b)
-                down_near = jnp.concatenate([down_near, other], axis=0)
-        down_far = swap(down_near, "c", nc, 1)
+                refs[nline][k * rows : (k + 1) * rows, :] = refs[k][...]
+
+        (got,) = call(stack, [((ffb, 3 * hc), BF)], (ranks, *w_got))
+        qkv_full = lax.all_gather(got, dpc, axis=0, tiled=True)
+
+        def stack_ff(rk, *refs):
+            parts, (wd, out) = refs[:nline], refs[nline:]
+            for k in range(nline):
+                out[k * rows : (k + 1) * rows, : 2 * ffq + dm] = parts[k][...]
+            out[:, 2 * ffq + dm :] = wd[...].astype(BF)
+
+        (got,) = call(
+            stack_ff,
+            [((ffb, 2 * ffq + 2 * dm), BF)],
+            (ranks, *ff_got, w_down),
+            after=(got,),
+        )
+        ff_full = lax.all_gather(got, dpc, axis=0, tiled=True)
 
         place = jnp.arange(nt, dtype=F32)[:, None]
         freq = 10000.0 ** (-jnp.arange(HEAD_DIM // 2, dtype=F32) / (HEAD_DIM // 2))
@@ -462,18 +475,14 @@
         table_hi = table.astype(BF)
         table_lo = (table - table_hi.astype(F32)).astype(BF)
 
-        def owner_copies(rk, near, far, dst, sems):
+        def natural(rk, src, cols, dst, sems):
             copies = []
-            for cr, src in enumerate((near, far)):
-                for a in range(nyx):
-                    for b in range(nline):
-                        row = ((rk[5] ^ a) * nline + (rk[6] ^ b)) * nc + (rk[4] ^ cr)
-                        row = pl.multiple_of(row * rows, 32)
-                        copies.append(
-                            pltpu.make_async_copy(
-                                src.at[a, b], dst.at[pl.ds(row, rows)], sems.at[len(copies)]
-                            )
-                        )
+            for b in range(ndpc):
+                for k in range(nline):
+                    row = ((b // nc) * nline + (rk[6] ^ k)) * nc + b % nc
+                    row = pl.ds(pl.multiple_of(row * rows, 32), rows)
+                    block = src.at[pl.ds((b * nline + k) * rows, rows), cols]
+                    copies.append(pltpu.make_async_copy(block, dst.at[row], sems.at[len(copies)]))
             return copies
 
         def heads_swap(v, low):
@@ -498,10 +507,10 @@
 
         def attn_forward(rk, *refs):
             ext_refs, refs = refs[:nline], refs[nline:]
-            near, far, gain, t_hi, t_lo = refs[:5]
-            att_outs, refs = refs[5 : 5 + nline], refs[5 + nline :]
+            stack, gain, t_hi, t_lo = refs[:4]
+            att_ref, refs = refs[4], refs[5:]
             x_ref, w_ref, rq_ref, rk_ref, q_ref, k_ref, v_ref, start_ref, cs_ref, sems = refs
-            copies = owner_copies(rk, near, far, w_ref, sems)
+            copies = natural(rk, stack, pl.ds(0, 3 * hc), w_ref, sems)
             for copy in copies:
                 copy.start()
             ids = []
@@ -544,98 +553,75 @@
                 s = jnp.where(allowed, s, NEG)
                 raw = jnp.exp(s - jnp.max(s, axis=1, keepdims=True))
                 p = raw * (1.0 / jnp.sum(raw, axis=1, keepdims=True))
-                att = dot(p.astype(BF), v_ref[:, at_h]).astype(BF)
-                for k in range(nline):
-                    att_outs[k][:, at_h] = att[k * tk : (k + 1) * tk]
+                att_ref[:, at_h] = dot(p.astype(BF), v_ref[:, at_h]).astype(BF)
 
         unit = ((nt, hc), BF)
         outs = call(
             attn_forward,
-            [((tk, hc), BF)] * nline
-            + [((nt, dm), BF), ((dm, 3 * hc), BF), ((nt, hc), F32), ((nt, hc), F32)]
+            [unit, ((nt, dm), BF), ((dm, 3 * hc), BF), ((nt, hc), F32), ((nt, hc), F32)]
             + [unit, unit, unit, ((nt, 128), F32), ((nt, 256), F32)],
-            (ranks, *pieces, qkv_near, qkv_far, my_gain, table_hi, table_lo),
-            hbm=(1 + nline, 2 + nline),
+            (ranks, *pieces, qkv_full, my_gain, table_hi, table_lo),
+            hbm=(1 + nline,),
             scratch=[pltpu.SemaphoreType.DMA((ndev,))],
             flops=2 * nt * dm * 3 * hc + 4 * nt * nt * hc,
         )
-        att_parts, outs = outs[:nline], outs[nline:]
-        x_all, qkv_full, r_q, r_k, q_low, k_low, v_low, start, cs = outs
-        att_got = exchange(att_parts, line, nline)
+        att, outs = outs[0], outs[1:]
+        x_all, w_qkv, r_q, r_k, q_low, k_low, v_low, start, cs = outs
+        att_got = gather(att, line, nline)
 
         def own_x(ext_ref):
             return jnp.concatenate([ext_ref[:seg], ext_ref[ext : ext + seg]], axis=0).astype(F32)
 
-        def attn_update(rk, *refs):
-            parts, refs = refs[:nline], refs[nline:]
-            near, far, ext_ref, alpha, low_ref, one_ref, raw_ref, w, sems = refs
-            copies = owner_copies(rk, near, far, w, sems)
-            for copy in copies:
-                copy.start()
-            for copy in copies:
-                copy.wait()
-            total = None
-            for k in range(nline):
-                w_k = w[pl.ds(pl.multiple_of((rk[6] ^ k) * hc, hc), hc), :]
-                term = dot(parts[k][...], w_k)
-                total = term if total is None else total + term
-            raw_ref[...] = total
-            x = own_x(ext_ref)
-            z = x + alpha[...] * (total * row_norm(total) - x)
-            one = z * row_norm(z)
-            one_ref[...] = one
-            low_ref[...] = one.astype(BF)
-
         alpha_a, alpha_m = alpha_attn.reshape(1, dm), alpha_mlp.reshape(1, dm)
         full = ((tk, dm), F32)
-        h_low, h_one, h_attn, full_out = call(
-            attn_update,
-            [((tk, dm), BF), full, full, ((dm, dm), BF)],
-            (ranks, *att_got, out_near, out_far, mine, alpha_a),
-            hbm=(1 + nline, 2 + nline),
-            scratch=[pltpu.SemaphoreType.DMA((ndev,))],
-            flops=2 * tk * dm * dm,
-        )
-
-        h_got = gather(h_low, quad, nquad)
-
-        def load_ff(rk, stack, near, far, scratch):
-            wug, wd, sems, sems_d = scratch
-            first, second = [], []
-            for b in range(nblk):
-                for k in range(nquad):
-                    row = pl.multiple_of(((rk[5] ^ k) * nblk + b) * rows, 32)
-                    src = stack.at[pl.ds((b * nquad + k) * rows, rows)]
-                    sem = sems.at[len(first)]
-                    first.append(pltpu.make_async_copy(src, wug.at[pl.ds(row, rows)], sem))
-            for cr, src in enumerate((near, far)):
-                for a in range(nline):
-                    peer = ((a % nw) * nz + a // nw) ^ rk[6]
-                    row = pl.multiple_of((peer * nc + (rk[4] ^ cr)) * ffb, 32)
-                    sem = sems_d.at[len(second)]
-                    second.append(pltpu.make_async_copy(src.at[a], wd.at[pl.ds(row, ffb)], sem))
-            return first, second
+
+        def load_out(rk, stack, wo, sems):
+            return natural(rk, stack, pl.ds(2 * ffq, dm), wo, sems)
+
+        def load_ff(rk, stack, scratch):
+            wug, wd, sems, sem_d = scratch
+            down = stack.at[:, pl.ds(2 * ffq + dm, dm)]
+            return (
+                natural(rk, stack, pl.ds(0, 2 * ffq), wug, sems),
+                [pltpu.make_async_copy(down, wd, sem_d.at[0])],
+            )
 
         w_scratch = [pltpu.VMEM((dm, 2 * ffq), BF), pltpu.VMEM((ffq, dm), BF)]
-        w_scratch += [pltpu.SemaphoreType.DMA((ndev,)), pltpu.SemaphoreType.DMA((nblk,))]
+        w_scratch += [pltpu.SemaphoreType.DMA((ndev,)), pltpu.SemaphoreType.DMA((1,))]
+        out_scratch = [pltpu.VMEM((dm, dm), BF), pltpu.SemaphoreType.DMA((ndev,))]
 
         def gate_terms(gate, sg):
             v = sg * gate
             s = 1.0 / (1.0 + jnp.exp(-v))
             return v, s
 
-        def ff_forward(rk, *refs):
-            h_refs, stacks = refs[:nquad], refs[nquad : nquad + 3]
-            su, sg = refs[nquad + 3 : nquad + 5]
-            refs = refs[nquad + 5 :]
-            parts, (h_all, up_ref, gate_ref, mixed_ref) = refs[:nquad], refs[nquad : nquad + 4]
-            scratch = refs[nquad + 4 :]
+        def forward(rk, *refs):
+            att_refs, refs = refs[:nline], refs[nline:]
+            x_ref, alpha, stack, su, sg = refs[:5]
+            parts, refs = refs[5 : 5 + nline], refs[5 + nline :]
+            h_all, up_ref, gate_ref, mixed_ref, one_ref, raw_ref = refs[:6]
+            scratch = refs[6:]
             wug, wd = scratch[:2]
-            first, third = load_ff(rk, *stacks, scratch)
-            for copy in first + third:
+            w = scratch[4]
+            first, third = load_ff(rk, stack, scratch[:4])
+            out_copies = load_out(rk, stack, w, scratch[5])
+            for copy in out_copies + first + third:
                 copy.start()
-            for k in range(nquad):
-                h_all[k * tk : (k + 1) * tk, :] = h_refs[k][...]
+            for copy in out_copies:
+                copy.wait()
+            for m in range(nline):
+                total = None
+                for k in range(nline):
+                    w_k = w[pl.ds(pl.multiple_of((rk[6] ^ k) * hc, hc), hc), :]
+                    term = dot(att_refs[k][(m ^ k) * tk : ((m ^ k) + 1) * tk, :], w_k)
+                    total = term if total is None else total + term
+                x = x_ref[m * tk : (m + 1) * tk, :].astype(F32)
+                z = x + alpha[...] * (total * row_norm(total) - x)
+                one = z * row_norm(z)
+                h_all[m * tk : (m + 1) * tk, :] = one.astype(BF)
+                if m == 0:
+                    one_ref[...] = one
+                    raw_ref[...] = total
             for copy in first:
                 copy.wait()
 
@@ -644,8 +630,8 @@
                 cols = pl.ds(pl.multiple_of(j * tile, tile), tile)
                 up = dot(h_all[...], wug[:, cols])
                 gate = dot(h_all[...], wug[:, pl.ds(pl.multiple_of(ffq + j * tile, tile), tile)])
-                up_ref[:, cols] = up
-                gate_ref[:, cols] = gate
+                up_ref[:, cols] = up.astype(BF)
+                gate_ref[:, cols] = gate.astype(BF)
                 v, s = gate_terms(gate, sg[:, cols])
                 mixed_ref[:, cols] = (su[:, cols] * up * (v * s)).astype(BF)
 
@@ -656,23 +642,21 @@
             def _(j):
                 cols = pl.ds(pl.multiple_of(j * tile, tile), tile)
                 part = dot(mixed_ref[...], wd[:, cols])
-                for k in range(nquad):
+                for k in range(nline):
                     parts[k][:, cols] = part[k * tk : (k + 1) * tk].astype(parts[k].dtype)
 
-        stacks = (ug_full, down_near, down_far)
-        part_shapes = [((tk, dm), F32)] + [((tk, dm), BF)] * (nquad - 1)
-        hbm = tuple(range(1 + nquad, 4 + nquad))
+        part_shapes = [((tk, dm), F32)] + [((tk, dm), BF)] * (nline - 1)
         outs = call(
-            ff_forward,
-            part_shapes + [((nt_q, dm), BF) for nt_q in (nquad * tk,)]
-            + [((nquad * tk, ffq), F32)] * 2 + [((nquad * tk, ffq), BF)],
-            (ranks, *h_got, *stacks, my_su, my_sg),
-            hbm=hbm,
-            scratch=w_scratch,
-            flops=6 * nquad * tk * dm * ffq,
-        )
-        mlp_parts, (h_all, up, gate, mixed) = outs[:nquad], outs[nquad:]
-        mlp_got = exchange(mlp_parts, quad, nquad)
+            forward,
+            part_shapes
+            + [((nt, dm), BF), ((nt, ffq), BF), ((nt, ffq), BF), ((nt, ffq), BF), full, full],
+            (ranks, *att_got, x_all, alpha_a, ff_full, my_su, my_sg),
+            hbm=(3 + nline,),
+            scratch=w_scratch + out_scratch,
+            flops=6 * nt * dm * ffq + 2 * nt * dm * dm,
+        )
+        mlp_parts, (h_all, up, gate, mixed, h_one, h_attn) = outs[:nline], outs[nline:]
+        mlp_got = exchange(mlp_parts, line, nline)
 
         def split_rows(rk, cot, keep, send):
             keep[...] = cot[rk[4]]
@@ -683,10 +667,10 @@
         cot_recv = swap(cot_send, "c", nc, 1)
 
         def mlp_update(rk, *refs):
-            parts, refs = refs[:nquad], refs[nquad:]
+            parts, refs = refs[:nline], refs[nline:]
             one_ref, alpha_ref, ck, cr, hid_keep, hid_send, dm_ref, direct, g_alpha = refs
             h = parts[0][...]
-            for k in range(1, nquad):
+            for k in range(1, nline):
                 h = h + parts[k][...].astype(F32)
             one, alpha = one_ref[...], alpha_ref[...]
             norm_h = row_norm(h)
@@ -711,19 +695,19 @@
         )
         hid_keep, hid_send, dm_low, d_one_direct, g_alpha_mlp = outs
         hid_recv = swap(hid_send, "c", nc, 1)
-        dm_got = gather(dm_low, quad, nquad)
+        dm_got = gather(dm_low, line, nline)
 
         def ff_back(rk, *refs):
-            d_refs, stacks = refs[:nquad], refs[nquad : nquad + 3]
-            su_ref, sg_ref, up_ref, gate_ref = refs[nquad + 3 : nquad + 7]
-            refs = refs[nquad + 7 :]
-            parts, (d_all, dug, g_su, g_sg) = refs[:nquad], refs[nquad : nquad + 4]
-            scratch = refs[nquad + 4 :]
+            d_refs, stack = refs[:nline], refs[nline]
+            su_ref, sg_ref, up_ref, gate_ref = refs[nline + 1 : nline + 5]
+            refs = refs[nline + 5 :]
+            parts, (d_all, dug, g_su, g_sg) = refs[:nline], refs[nline : nline + 4]
+            scratch = refs[nline + 4 :]
             wug, wd = scratch[:2]
-            first, third = load_ff(rk, *stacks, scratch)
+            first, third = load_ff(rk, stack, scratch)
             for copy in third + first:
                 copy.start()
-            for k in range(nquad):
+            for k in range(nline):
                 d_all[k * tk : (k + 1) * tk, :] = d_refs[k][...]
             for copy in third:
                 copy.wait()
@@ -732,7 +716,7 @@
             def _(j):
                 cols = pl.ds(pl.multiple_of(j * tile, tile), tile)
                 d_mixed = dot_t(d_all[...], wd[cols, :])
-                up, gate = up_ref[:, cols], gate_ref[:, cols]
+                up, gate = up_ref[:, cols].astype(F32), gate_ref[:, cols].astype(F32)
                 su, sg = su_ref[:, cols], sg_ref[:, cols]
                 v, s = gate_terms(gate, sg)
                 silu = v * s
@@ -750,103 +734,72 @@
             def _(j):
                 cols = pl.ds(pl.multiple_of(j * tile, tile), tile)
                 part = dot_t(dug[...], wug[cols, :])
-                for k in range(nquad):
+                for k in range(nline):
                     parts[k][:, cols] = part[k * tk : (k + 1) * tk].astype(parts[k].dtype)
 
         outs = call(
             ff_back,
-            part_shapes + [((nquad * tk, dm), BF), ((nquad * tk, 2 * ffq), BF)] + [((1, ffq), F32)] * 2,
-            (ranks, *dm_got, *stacks, my_su, my_sg, up, gate),
-            hbm=hbm,
+            part_shapes + [((nline * tk, dm), BF), ((nline * tk, 2 * ffq), BF)] + [((1, ffq), F32)] * 2,
+            (ranks, *dm_got, ff_full, my_su, my_sg, up, gate),
+            hbm=(1 + nline,),
             scratch=w_scratch,
-            flops=6 * nquad * tk * dm * ffq,
-        )
-        one_parts, (dm_all, dug_low, g_su, g_sg) = outs[:nquad], outs[nquad:]
-        one_got = exchange(one_parts, quad, nquad)
-
-        def store_blocks(scratch, outs, rows_of, count, depth, sems):
-            copies = []
-            for i, out in enumerate(outs):
-                for r in range(count):
-                    src = scratch.at[pl.ds(pl.multiple_of(rows_of(i, r) * depth, 32), depth)]
-                    copies.append(pltpu.make_async_copy(src, out.at[r], sems.at[len(copies)]))
-            return copies
-
-        def down_row(rk, cr, r):
-            peer = ((r % nw) * nz + r // nw) ^ rk[6]
-            return peer * nc + (rk[4] ^ cr)
-
-        def ff_row(rk, part, r):
-            return (rk[5] ^ (r % nquad)) * nblk + r // nquad
-
-        def own_row(rk, cr, r):
-            return ((rk[5] ^ (r // nline)) * nline + (rk[6] ^ (r % nline))) * nc + (rk[4] ^ cr)
-
-        def outer(row_of, count, depth, nout=2):
-            def kernel(rk, left, right, *refs):
-                outs, (g_ref, sems) = refs[:nout], refs[nout:]
-                height = left.shape[1]
-
-                @pl.loop(0, height // tile)
-                def _(j):
-                    cols = pl.ds(pl.multiple_of(j * tile, tile), tile)
-                    g_ref[cols, :] = tdot(left[:, cols], right[...]).astype(BF)
-
-                copies = store_blocks(
-                    g_ref, outs, lambda i, r: row_of(rk, i, r), count, depth, sems
-                )
-                for copy in copies:
-                    copy.start()
-                for copy in copies:
-                    copy.wait()
-
-            def run(left, right):
-                shape = ((count, depth, right.shape[1]), BF)
-                return call(
-                    kernel,
-                    [shape] * nout,
-                    (ranks, left, right),
-                    hbm_out=tuple(range(nout)),
-                    scratch=[
-                        pltpu.VMEM((left.shape[1], right.shape[1]), BF),
-                        pltpu.SemaphoreType.DMA((nout * count,)),
-                    ],
-                    flops=2 * left.shape[0] * left.shape[1] * right.shape[1],
-                )
-
-            return run
-
-        def add(a, b):
-            return a.astype(F32) + b.astype(F32)
-
-        keep, send = outer(down_row, nline, ffb)(mixed, dm_all)
-        total = add(keep, swap(send, "c", nc, 1))
-        for axis, count in (("z", nz), ("w", nw)):
-            for b in reversed(range(count.bit_length() - 1)):
-                half = total.shape[0] // 2
-                total = add(total[:half], swap(total[half:].astype(BF), axis, count, 1 << b))
-        g_down = total[0]
-
-        (g_ug,) = outer(ff_row, nblk * nquad, rows, 1)(h_all, dug_low)
-        g_ug = g_ug.reshape(dm, 2 * ffq)
-        g_ug = lax.psum_scatter(g_ug, blk, scatter_dimension=0, tiled=True)
-        g_parts = exchange([g_ug[k * rows : (k + 1) * rows] for k in range(nquad)], quad, nquad)
-
-        def place_ff(rk, *refs):
-            parts, outs = refs[:nquad], refs[nquad:]
-            for k in range(nquad):
-                cols = pl.ds(pl.multiple_of((rk[5] ^ k) * ffq, 128), ffq)
-                for i in range(2):
-                    outs[i][:, cols] = parts[k][:, i * ffq : (i + 1) * ffq].astype(F32)
-
-        g_up, g_gate = call(place_ff, [((rows, ff), F32)] * 2, (ranks, *g_parts))
-
+            flops=6 * nline * tk * dm * ffq,
+        )
+        one_parts, (dm_all, dug_low, g_su, g_sg) = outs[:nline], outs[nline:]
+        one_got = exchange(one_parts, line, nline)
+
+        def stored(rk, g_ref, out, width, block, sems):
+            d, peer, c = block // (nline * nc), (block // nc) % nline, block % nc
+            spot = ((d * nc + c) * nline + (peer ^ rk[6])) * rows
+            src = g_ref.at[pl.ds(pl.multiple_of(block * rows, 32), rows)]
+            dst = out.at[pl.ds(pl.multiple_of(spot, 32), rows), pl.ds(0, width)]
+            return pltpu.make_async_copy(src, dst, sems.at[block])
+
+        def outer_ff(rk, h, dug, mixed_ref, d_all, out, g_ref, g_down_ref, sems, sem_d):
+            def store(block):
+                return stored(rk, g_ref, out, 2 * ffq, block, sems)
+
+            @pl.loop(0, dm // tile)
+            def _(j):
+                cols = pl.ds(pl.multiple_of(j * tile, tile), tile)
+                g_ref[cols, :] = tdot(h[:, cols], dug[...]).astype(BF)
+                for i in range(tile // rows):
+                    store(j * (tile // rows) + i).start()
+
+            @pl.loop(0, ffq // tile)
+            def _(j):
+                cols = pl.ds(pl.multiple_of(j * tile, tile), tile)
+                g_down_ref[cols, :] = tdot(mixed_ref[:, cols], d_all[...]).astype(BF)
+
+            down = pltpu.make_async_copy(g_down_ref, out.at[:, pl.ds(2 * ffq, dm)], sem_d.at[0])
+            down.start()
+            down.wait()
+
+            @pl.loop(0, ndev)
+            def _(block):
+                store(block).wait()
+
+        (g_ff,) = call(
+            outer_ff,
+            [((dm, 2 * ffq + dm), BF)],
+            (ranks, h_all, dug_low, mixed, dm_all),
+            hbm_out=(0,),
+            scratch=[
+                pltpu.VMEM((dm, 2 * ffq), BF), pltpu.VMEM((ffq, dm), BF),
+                pltpu.SemaphoreType.DMA((ndev,)), pltpu.SemaphoreType.DMA((1,)),
+            ],
+            flops=6 * nt * dm * ffq,
+        )
+        g_ff = lax.psum_scatter(g_ff, dpc, scatter_dimension=0, tiled=True)
         def attn_update_back(rk, *refs):
-            parts, refs = refs[:nquad], refs[nquad:]
-            direct_in, one_ref, raw_ref, ext_ref, alpha_ref, w = refs[:6]
-            d_outs, (dh_ref, direct, g_alpha) = refs[6 : 6 + nline], refs[6 + nline :]
+            parts, refs = refs[:nline], refs[nline:]
+            direct_in, one_ref, raw_ref, ext_ref, alpha_ref, stack = refs[:6]
+            d_outs, (dh_ref, direct, g_alpha, w, sems) = refs[6 : 6 + nline], refs[6 + nline :]
+            copies = load_out(rk, stack, w, sems)
+            for copy in copies:
+                copy.start()
             d = direct_in[...] + parts[0][...]
-            for k in range(1, nquad):
+            for k in range(1, nline):
                 d = d + parts[k][...].astype(F32)
             one, raw, alpha = one_ref[...], raw_ref[...], alpha_ref[...]
             x = own_x(ext_ref)
@@ -858,6 +811,8 @@
             g_alpha[...] = jnp.sum(dz * gap, axis=0, keepdims=True)
             direct[...] = dz * (1.0 - alpha)
             dh_ref[...] = sphere_back(dz * alpha, b, norm_raw).astype(BF)
+            for copy in copies:
+                copy.wait()
             for k in range(nline):
                 w_k = w[pl.ds(pl.multiple_of((rk[6] ^ k) * hc, hc), hc), :]
                 d_outs[k][...] = dot_t(dh_ref[...], w_k).astype(BF)
@@ -865,7 +820,9 @@
         outs = call(
             attn_update_back,
             [((tk, hc), BF)] * nline + [((tk, dm), BF), full, ((1, dm), F32)],
-            (ranks, *one_got, d_one_direct, h_one, h_attn, mine, alpha_a, full_out),
+            (ranks, *one_got, d_one_direct, h_one, h_attn, mine, alpha_a, ff_full),
+            hbm=(6 + nline,),
+            scratch=out_scratch,
             flops=2 * tk * dm * dm,
         )
         d_att_parts, (dh_low, d_x_direct, g_alpha_attn) = outs[:nline], outs[nline:]
@@ -922,7 +879,7 @@
             attn_back,
             [((tk, dm), F32)] + [((tk, dm), BF)] * (nline - 1)
             + [((nt, 3 * hc), BF), ((1, hc), F32)],
-            (ranks, *d_att, qkv_full, r_q, r_k, q_low, k_low, v_low, start, cs, my_gain),
+            (ranks, *d_att, w_qkv, r_q, r_k, q_low, k_low, v_low, start, cs, my_gain),
             scratch=[
                 pltpu.VMEM((nt, hc), BF), pltpu.VMEM((nt, hc), F32), pltpu.VMEM((nt, hc), F32)
             ],
@@ -951,85 +908,110 @@
         (tokens_grad,) = call(join_rows, [((nseq, seg, dm), F32)], (ranks, x_keep, x_recv))
         (hidden_out,) = call(join_rows, [((nseq, seg, dm), BF)], (ranks, hid_keep, hid_recv))
 
-        def sum_over(chunks, axes, count):
-            got = exchange([chunks[0]] + [c.astype(BF) for c in chunks[1:]], axes, count)
-            total = got[0].astype(F32)
-            for piece in got[1:]:
-                total = total + piece.astype(F32)
-            return total
-
-        def outer_out(rk, *refs):
-            parts, (dh, keep, send, g_ref, sems) = refs[:nline], refs[nline:]
+        at_line = ranks[6]
+        mine_ff = (jnp.arange(nline) == at_line)[None, :, None, None]
+
+        def ff_owner(vec):
+            return jnp.where(mine_ff, vec.reshape(nyx, 1, nc, ffb), 0.0).reshape(ndev, ffb)
+
+        gains = jnp.where((jnp.arange(nyx) == at_line)[:, None], g_gain, 0.0)
+        misc = [v.reshape(ndev, rows) for v in (g_alpha_attn, g_alpha_mlp, gains)]
+        misc = jnp.pad(jnp.concatenate(misc, axis=1), ((0, 0), (0, ffb - 3 * rows)))
+        vecs = jnp.stack([ff_owner(g_su), ff_owner(g_sg), misc], axis=1).astype(BF)
+        vecs = jnp.pad(vecs, ((0, 0), (0, rows - 3), (0, 0))).reshape(dm, ffb)
+
+        wide = 3 * hc + ffb
+
+        def outer_last(rk, x_ref, d_ref, vec_ref, dh, *refs):
+            parts, (out, g_ref, sems) = refs[:nline], refs[nline:]
+
+            def store(block):
+                return stored(rk, g_ref, out, wide + dm, block, sems)
+
             for k in range(nline):
                 spot = pl.ds(pl.multiple_of((rk[6] ^ k) * hc, hc), hc)
-                g_ref[spot, :] = tdot(parts[k][...], dh[...]).astype(BF)
-            copies = store_blocks(
-                g_ref, (keep, send), lambda i, r: own_row(rk, i, r), nyx * nline, rows, sems
-            )
-            for copy in copies:
-                copy.start()
-            for copy in copies:
-                copy.wait()
-
-        shape = ((nyx * nline, rows, dm), BF)
-        keep, send = call(
-            outer_out,
-            [shape, shape],
-            (ranks, *att_got, dh_low),
-            hbm_out=(0, 1),
-            scratch=[pltpu.VMEM((dm, dm), BF), pltpu.SemaphoreType.DMA((2 * nyx * nline,))],
-            flops=2 * tk * dm * dm,
-        )
-
-        def across(keep, send):
-            total = add(keep, swap(send, "c", nc, 1))
-            total = total.reshape((nyx, nline) + total.shape[1:])
-            return sum_over([total[k] for k in range(nyx)], yx, nyx)
-
-        total = across(keep, send)
-        g_out = sum_over([total[k] for k in range(nline)], line, nline)
-        total = across(*outer(own_row, nyx * nline, rows)(x_all, d_qkv)).astype(BF)
-        got = exchange([total[k] for k in range(nline)], line, nline)
-
-        def place_qkv(rk, *refs):
-            parts, outs = refs[:nline], refs[nline:]
+                own = parts[k][k * tk : (k + 1) * tk, :]
+                g_ref[spot, wide:] = tdot(own, dh[...]).astype(BF)
+            g_ref[:, 3 * hc : wide] = vec_ref[...]
+
+            @pl.loop(0, dm // tile)
+            def _(j):
+                cols = pl.ds(pl.multiple_of(j * tile, tile), tile)
+                g_ref[cols, : 3 * hc] = tdot(x_ref[:, cols], d_ref[...]).astype(BF)
+                for i in range(tile // rows):
+                    store(j * (tile // rows) + i).start()
+
+            @pl.loop(0, ndev)
+            def _(block):
+                store(block).wait()
+
+        (g_last,) = call(
+            outer_last,
+            [((dm, wide + dm), BF)],
+            (ranks, x_all, d_qkv, vecs, dh_low, *att_got),
+            hbm_out=(0,),
+            scratch=[pltpu.VMEM((dm, wide + dm), BF), pltpu.SemaphoreType.DMA((ndev,))],
+            flops=2 * nt * dm * 3 * hc,
+        )
+        g_last = lax.psum_scatter(g_last, dpc, scatter_dimension=0, tiled=True)
+
+        def split_ff(rk, g_ref, down, *outs):
+            down[...] = g_ref[:, 2 * ffq :].astype(F32)
+            for k in range(nline):
+                outs[k][...] = g_ref[k * rows : (k + 1) * rows, : 2 * ffq]
+
+        g_down, *g_parts = call(
+            split_ff,
+            [((ffb, dm), F32)] + [((rows, 2 * ffq), BF)] * nline,
+            (ranks, g_ff),
+            after=tuple(x_got[1:]),
+        )
+        g_parts = exchange(g_parts, line, nline)
+
+        def split_last(rk, g_ref, *outs):
+            for k in range(nline):
+                outs[k][...] = g_ref[k * rows : (k + 1) * rows, :]
+
+        last = call(
+            split_last,
+            [((rows, wide + dm), BF)] * nline,
+            (ranks, g_last),
+            after=tuple(g_parts[1:]),
+        )
+        last = exchange(last, line, nline)
+
+        def place_last(rk, *refs):
+            parts, ff_parts = refs[:nline], refs[nline : 2 * nline]
+            outs, refs = refs[2 * nline : 2 * nline + 3], refs[2 * nline + 3 :]
+            g_o, ff_outs, vec_outs = refs[0], refs[1:3], refs[3:]
+            g_sum, v_sum = None, None
             for k in range(nline):
                 cols = pl.ds(pl.multiple_of((rk[6] ^ k) * hc, 128), hc)
                 for i in range(3):
                     outs[i][:, cols] = parts[k][:, i * hc : (i + 1) * hc].astype(F32)
-
-        g_query, g_key, g_value = call(place_qkv, [((rows, dm), F32)] * 3, (ranks, *got))
-
-        width = 2 * ffb + 3 * rows
-
-        def spread(vec, rank, count):
-            return jnp.where(jnp.arange(count)[:, None] == rank, vec[None], 0.0)
-
-        def ff_order(vec):
-            return spread(vec, ranks[5], nquad).reshape(ndev, ffb)
-
-        at_line = ranks[6]
-        vecs = jnp.concatenate(
-            [
-                spread(g_gain[0], at_line, nline).reshape(ndev, -1),
-                g_alpha_attn.reshape(ndev, -1),
-                ff_order(g_su[0]),
-                ff_order(g_sg[0]),
-                g_alpha_mlp.reshape(ndev, -1),
-            ],
-            axis=1,
-        )
-        order = (
-            (jnp.arange(nc)[:, None, None] ^ at[4])
-            + nc * (jnp.arange(nline)[None, None, :] ^ at_line)
-            + nc * nline * (jnp.arange(nyx)[None, :, None] ^ ranks[5])
-        ).reshape(-1)
-        vecs = jnp.take(vecs, order, axis=0).reshape(nc, nyx, nline, width)
-        vecs = vecs[0] + swap(vecs[1], "c", nc, 1)
-        vecs = sum(exchange([vecs[k] for k in range(nyx)], yx, nyx))
-        vecs = sum(exchange([vecs[k] for k in range(nline)], line, nline))
-        cuts = [rows, 2 * rows, 2 * rows + ffb, 2 * rows + 2 * ffb]
-        g_sqk, g_aa, g_s_up, g_s_gate, g_am = jnp.split(vecs, cuts)
+                vec = parts[k][:16, 3 * hc : wide].astype(F32)
+                part = parts[k][:, wide:].astype(F32)
+                for d, cols in enumerate(ff_cols(rk, k)):
+                    for i in range(2):
+                        here = i * ffq + d * sub
+                        ff_outs[i][:, cols] = ff_parts[k][:, here : here + sub].astype(F32)
+                g_sum = part if g_sum is None else g_sum + part
+                v_sum = vec if v_sum is None else v_sum + vec
+            g_o[...] = g_sum
+            vec_outs[0][...] = v_sum[:1]
+            vec_outs[1][...] = v_sum[1:2]
+            for i in range(3):
+                vec_outs[2 + i][...] = v_sum[2:3, i * rows : (i + 1) * rows]
+
+        g_query, g_key, g_value, g_out, g_up, g_gate, *vecs = call(
+            place_last,
+            [((rows, dm), F32)] * 4
+            + [((rows, ff), F32)] * 2
+            + [((1, ffb), F32)] * 2
+            + [((1, rows), F32)] * 3,
+            (ranks, *last, *g_parts),
+        )
+        g_s_up, g_s_gate, g_aa, g_am, g_sqk = [v.reshape(-1) for v in vecs]
         return (
             hidden_out, tokens_grad, g_query, g_key, g_value, g_out, g_up, g_gate, g_down,
             g_sqk, g_aa, g_s_up, g_s_gate, g_am,

time: 403 us -> 353 us (0.88)
  starting transfers between devices: 118 us -> 68.2 us
  waiting for transfers between devices: 129 us -> 153 us
  other arithmetic: 17.5 us -> 4.84 us
  local copies, waits for them, and re-layouts: 20.7 us -> 14.7 us
  Pallas kernels: 101 us -> 96.4 us
    ppermute x75 -> x37, starting transfers between devices: 118 us -> 68 us  [swap(): return lax.ppermute(value, axes, [(i, i ^ k) for i in range(count)])]
    reduce_scatter x1 -> x2, waiting for transfers between devices: 0.01 us -> 18.5 us  [the longest x1 18.5 us: body(): g_last = lax.psum_scatter(g_last, dpc, scatter_dimension=0, tiled=True)]
    ppermute x75 -> x37, waiting for transfers between devices: 129 us -> 135 us  [swap(): return lax.ppermute(value, axes, [(i, i ^ k) for i in range(count)])]
    pallas_call x21 -> x19, Pallas kernels: 101 us -> 96.4 us  [call(): pl.pallas_call(run, out_shape=[jax.ShapeDtypeStruct(s, d) for s, d in out...]
    unnamed x99 -> x100, local copies, waits for them, and re-layouts: 8.66 us -> 10.6 us
  transfers between devices with their start and end apart: 77 -> 41, of which waited for: 36 -> 23; matrix products, arithmetic and copies ran while one was open for 6% -> 2% of each run, Pallas kernels for 15% -> 14%
where the time goes in v1:
time: 353 us; the launch traced here: 352 us
  waiting for transfers between devices  153 us (43%)
  Pallas kernels  96.4 us (27%)
  starting transfers between devices  68.2 us (19%)
  local copies, waits for them, and re-layouts  14.7 us (4%)
  between operations  14.2 us (4%)
  other arithmetic  4.84 us (1%)
    ppermute x37, waiting for transfers between devices, swap(): return lax.ppermute(value, axes, [(i, i ^ k) for i in range(count)])  135 us
    pallas_call x19, Pallas kernels, call(): pl.pallas_call(run, out_shape=[jax.ShapeDtypeStruct(s, d) for s, d in out...  96.4 us
    ppermute x37, starting transfers between devices, swap(): return lax.ppermute(value, axes, [(i, i ^ k) for i in range(count)])  68 us
    reduce_scatter x1, waiting for transfers between devices, body(): g_last = lax.psum_scatter(g_last, dpc, scatter_dimension=0, tiled=True)  18.5 us
    unnamed x100, local copies, waits for them, and re-layouts  10.6 us
  transfers between devices with their start and end apart: 41, of which 23 were waited for; matrix products, arithmetic and copies ran while one was open for 2% of the time, Pallas kernels for 14%

profile of v1, /device:TPU:0, one launch (start us, length us, event | category | flops | bytes accessed | tf_op | source)
XLA Modules:
  0.0 351.7 jit_solution(6860295630049397933)
XLA Ops:
  13.4 3.1 collective-permute-start.4
  19.1 3.5 %collective-permute-done.5.refs_3_ = bf16[32,768]{1,0:T(8,128)(2,1)S(1)} collective-permute-done((bf16[32,768]{1,0:T(8,128)(2,1)}, bf16[32,768]{1,0:T(8,128)(2,1)S(1)}, u32[]{:S(2)}, u32[]{:S(2)}) %collective-permute-start.5) | collective-permute-done | bytes 49184 | tf_op jit(solution)/shard_map/ppermute | solution.py:366
  28.8 3.1 collective-permute-start.12
  31.9 4.8 %collective-permute-done.10.refs_2_ = bf16[32,3072]{1,0:T(8,128)(2,1)S(1)} collective-permute-done((bf16[32,3072]{1,0:T(8,128)(2,1)}, bf16[32,3072]{1,0:T(8,128)(2,1)S(1)}, u32[]{:S(2)}, u32[]{:S(2)}) %collective-permute-start.10) | collective-permute-done | bytes 196640 | tf_op jit(solution)/shard_map/ppermute | solution.py:366
  36.7 7.3 %collective-permute-done.11.refs_3_ = bf16[32,3072]{1,0:T(8,128)(2,1)S(1)} collective-permute-done((bf16[32,3072]{1,0:T(8,128)(2,1)}, bf16[32,3072]{1,0:T(8,128)(2,1)S(1)}, u32[]{:S(2)}, u32[]{:S(2)}) %collective-permute-start.11) | collective-permute-done | bytes 196640 | tf_op jit(solution)/shard_map/ppermute | solution.py:366
  57.1 8.5 %collective-permute-done.1.refs_2_ = bf16[160,1024]{1,0:T(8,128)(2,1)S(1)} collective-permute-done((bf16[160,1024]{1,0:T(8,128)(2,1)S(1)}, bf16[160,1024]{1,0:T(8,128)(2,1)S(1)}, u32[]{:S(2)}, u32[]{:S(2)}) %collective-permute-start.1) | collective-permute-done | bytes 327712 | tf_op jit(solution)/shard_map/ppermute | solution.py:366
  65.6 11.8 %collective-permute-done.2.refs_3_ = bf16[160,1024]{1,0:T(8,128)(2,1)S(1)} collective-permute-done((bf16[160,1024]{1,0:T(8,128)(2,1)S(1)}, bf16[160,1024]{1,0:T(8,128)(2,1)S(1)}, u32[]{:S(2)}, u32[]{:S(2)}) %collective-permute-start.2) | collective-permute-done | bytes 327712 | tf_op jit(solution)/shard_map/ppermute | solution.py:366
  78.2 10.2 %shard_map.257 = (bf16[512,256]{1,0:T(8,128)(2,1)}, bf16[512,1024]{1,0:T(8,128)(2,1)}, bf16[1024,768]{1,0:T(8,128)(2,1)}, f32[512,256]{1,0:T(8,128)}, f32[512,25...) custom-call(s32[7]{0:T(128)} %stack.39.refs_0_, ...), custom_call_target="tpu_custom_call" | custom-call | flops 1073741824 | bytes 8913948 | tf_op jit(solution)/shard_map/pallas_call | solution.py:339
  88.5 6.5 %collective-permute-start.7 = (bf16[512,256]{1,0:T(8,128)(2,1)}, bf16[512,256]{1,0:T(8,128)(2,1)S(1)}, u32[]{:S(2)}, u32[]{:S(2)}) collective-permute-start(bf16[512,256]{1,0:T(8,128)(2,1)} %get-tuple-element.104.refs_1_.refs_5_), channel_id=1, source_target_pairs={{0,2},{2,0},{4,6},{6,4},{1,3},{3,1},{5,7},{7,5},{8,10},{10,8},{12,... | collective-permute-start | bytes 786440 | tf_op jit(solution)/shard_map/ppermute | solution.py:366
  97.4 7.9 %collective-permute-done.7.refs_2_.refs_6_ = bf16[512,256]{1,0:T(8,128)(2,1)S(1)} collective-permute-done((bf16[512,256]{1,0:T(8,128)(2,1)}, bf16[512,256]{1,0:T(8,128)(2,1)S(1)}, u32[]{:S(2)}, u32[]{:S(2)}) %collective-permute-start.7) | collective-permute-done | bytes 262176 | tf_op jit(solution)/shard_map/ppermute | solution.py:366
  105.3 11.2 %collective-permute-done.8.refs_3_.refs_7_ = bf16[512,256]{1,0:T(8,128)(2,1)S(1)} collective-permute-done((bf16[512,256]{1,0:T(8,128)(2,1)}, bf16[512,256]{1,0:T(8,128)(2,1)S(1)}, u32[]{:S(2)}, u32[]{:S(2)}) %collective-permute-start.8) | collective-permute-done | bytes 262176 | tf_op jit(solution)/shard_map/ppermute | solution.py:366
  117.4 14.0 %shard_map.259 = (f32[128,1024]{1,0:T(8,128)}, bf16[128,1024]{1,0:T(8,128)(2,1)}, bf16[128,1024]{1,0:T(8,128)(2,1)}, bf16[128,1024]{1,0:T(8,128)(2,1)}, bf16[512...) custom-call(s32[7]{0:T(128)} %stack.39.refs_0_, ...), custom_call_target="tpu_custom_call" | custom-call | flops 4294967296 | bytes 17051676 | tf_op jit(solution)/shard_map/pallas_call | solution.py:339
  131.4 4.4 %collective-permute-start.13 = (bf16[128,1024]{1,0:T(8,128)(2,1)}, bf16[128,1024]{1,0:T(8,128)(2,1)S(1)}, u32[]{:S(2)}, u32[]{:S(2)}) collective-permute-start(bf16[128,1024]{1,0:T(8,128)(2,1)} %get-tuple-element.113), channel_id=1, source_target_pairs={{0,2},{2,0},{4,6},{6,4},{1,3},{3,1},{5,7},{7,5},{8,10},{10,8},{12,... | collective-permute-start | bytes 786440 | tf_op jit(solution)/shard_map/ppermute | solution.py:366
  141.5 3.7 %collective-permute-done.13.refs_2_ = bf16[128,1024]{1,0:T(8,128)(2,1)S(1)} collective-permute-done((bf16[128,1024]{1,0:T(8,128)(2,1)}, bf16[128,1024]{1,0:T(8,128)(2,1)S(1)}, u32[]{:S(2)}, u32[]{:S(2)}) %collective-permute-start.13) | collective-permute-done | bytes 262176 | tf_op jit(solution)/shard_map/ppermute | solution.py:366
  145.1 11.3 %collective-permute-done.14.refs_3_ = bf16[128,1024]{1,0:T(8,128)(2,1)S(1)} collective-permute-done((bf16[128,1024]{1,0:T(8,128)(2,1)}, bf16[128,1024]{1,0:T(8,128)(2,1)S(1)}, u32[]{:S(2)}, u32[]{:S(2)}) %collective-permute-start.14) | collective-permute-done | bytes 262176 | tf_op jit(solution)/shard_map/ppermute | solution.py:366
  160.2 4.2 %collective-permute-start.18 = (bf16[128,1024]{1,0:T(8,128)(2,1)}, bf16[128,1024]{1,0:T(8,128)(2,1)S(1)}, u32[]{:S(2)}, u32[]{:S(2)}) collective-permute-start(bf16[128,1024]{1,0:T(8,128)(2,1)} %get-tuple-element.121.refs_1_), channel_id=1, source_target_pairs={{0,2},{2,0},{4,6},{6,4},{1,3},{3,1},{5,7},{7,5},{8,10},{10,8},{12,... | collective-permute-start | bytes 786440 | tf_op jit(solution)/shard_map/ppermute | solution.py:366
  166.8 6.8 %collective-permute-done.18.refs_2_ = bf16[128,1024]{1,0:T(8,128)(2,1)S(1)} collective-permute-done((bf16[128,1024]{1,0:T(8,128)(2,1)}, bf16[128,1024]{1,0:T(8,128)(2,1)S(1)}, u32[]{:S(2)}, u32[]{:S(2)}) %collective-permute-start.18) | collective-permute-done | bytes 262176 | tf_op jit(solution)/shard_map/ppermute | solution.py:366
  173.6 10.9 %collective-permute-done.19.refs_3_ = bf16[128,1024]{1,0:T(8,128)(2,1)S(1)} collective-permute-done((bf16[128,1024]{1,0:T(8,128)(2,1)}, bf16[128,1024]{1,0:T(8,128)(2,1)S(1)}, u32[]{:S(2)}, u32[]{:S(2)}) %collective-permute-start.19) | collective-permute-done | bytes 262176 | tf_op jit(solution)/shard_map/ppermute | solution.py:366
  185.4 12.9 %shard_map.263 = (f32[128,1024]{1,0:T(8,128)}, bf16[128,1024]{1,0:T(8,128)(2,1)}, bf16[128,1024]{1,0:T(8,128)(2,1)}, bf16[128,1024]{1,0:T(8,128)(2,1)}, bf16[512...) custom-call(s32[7]{0:T(128)} %stack.39.refs_0_, ...), custom_call_target="tpu_custom_call" | custom-call | flops 3221225472 | bytes 16007196 | tf_op jit(solution)/shard_map/pallas_call | solution.py:339
  198.2 9.2 %shard_map.269 = bf16[1024,3072]{1,0:T(8,128)(2,1)} custom-call(s32[7]{0:T(128)} %stack.39.refs_0_, bf16[512,1024]{1,0:T(8,128)(2,1)} %get-tuple-element.156.refs_1_, bf16[512,2048]{1,0:T(8,128)(2,1)} %get-tuple-element.157.refs_2_, bf16[512,1024]{1,0:T(8,128)(2,1)} %get-tuple-element.158.refs_3_, bf16[512,1024]{1,0:T(8,128)(2,1)} %get-tuple-element.159.refs_4_), custom_call_target="tpu_custom_call" | custom-call | flops 3221225472 | bytes 11534364 | tf_op jit(solution)/shard_map/pallas_call | solution.py:339
  208.4 4.4 %collective-permute-start.21 = (bf16[128,1024]{1,0:T(8,128)(2,1)S(1)}, bf16[128,1024]{1,0:T(8,128)(2,1)S(1)}, u32[]{:S(2)}, u32[]{:S(2)}) collective-permute-start(bf16[128,1024]{1,0:T(8,128)(2,1)S(1)} %copy-done.40), channel_id=1, source_target_pairs={{0,2},{2,0},{4,6},{6,4},{1,3},{3,1},{5,7},{7,5},{8,10},{10,8},{12,... | collective-permute-start | bytes 786440 | tf_op jit(solution)/shard_map/ppermute | solution.py:366
  215.5 6.1 %collective-permute-done.21.refs_2_ = bf16[128,1024]{1,0:T(8,128)(2,1)S(1)} collective-permute-done((bf16[128,1024]{1,0:T(8,128)(2,1)S(1)}, bf16[128,1024]{1,0:T(8,128)(2,1)S(1)}, u32[]{:S(2)}, u32[]{:S(2)}) %collective-permute-start.21) | collective-permute-done | bytes 262176 | tf_op jit(solution)/shard_map/ppermute | solution.py:366
  221.6 11.7 %collective-permute-done.22.refs_3_ = bf16[128,1024]{1,0:T(8,128)(2,1)S(1)} collective-permute-done((bf16[128,1024]{1,0:T(8,128)(2,1)S(1)}, bf16[128,1024]{1,0:T(8,128)(2,1)S(1)}, u32[]{:S(2)}, u32[]{:S(2)}) %collective-permute-start.22) | collective-permute-done | bytes 262176 | tf_op jit(solution)/shard_map/ppermute | solution.py:366
  234.0 5.3 %shard_map.264 = (bf16[128,256]{1,0:T(8,128)(2,1)}, bf16[128,256]{1,0:T(8,128)(2,1)}, bf16[128,256]{1,0:T(8,128)(2,1)}, bf16[128,256]{1,0:T(8,128)(2,1)}, bf16[1...) custom-call(s32[7]{0:T(128)} %stack.39.refs_0_, f32[128,1024]{1,0:T(8,128)} %get-tuple-element.124.refs_1_, ...), custom_call_target="tpu_custom_call" | custom-call | flops 268435456 | bytes 12656668 | tf_op jit(solution)/shard_map/pallas_call | solution.py:339
  239.3 4.2 %collective-permute-start.24 = (bf16[128,256]{1,0:T(8,128)(2,1)}, bf16[128,256]{1,0:T(8,128)(2,1)S(1)}, u32[]{:S(2)}, u32[]{:S(2)}) collective-permute-start(bf16[128,256]{1,0:T(8,128)(2,1)} %get-tuple-element.131), channel_id=1, source_target_pairs={{0,2},{2,0},{4,6},{6,4},{1,3},{3,1},{5,7},{7,5},{8,10},{10,8},{12,... | collective-permute-start | bytes 196616 | tf_op jit(solution)/shard_map/ppermute | solution.py:366
  250.5 13.8 %shard_map.265 = (f32[128,1024]{1,0:T(8,128)}, bf16[128,1024]{1,0:T(8,128)(2,1)}, bf16[128,1024]{1,0:T(8,128)(2,1)}, bf16[128,1024]{1,0:T(8,128)(2,1)}, bf16[512,768]{1,0:T(8,128)(2,1)}, /*index=5*/f32[1,256]{1,0:T(1,128)}) custom-call(s32[7]{0:T(128)} %stack.39.refs_0_, bf16[128,256]{1,0:T(8,128)(2,1)} %get-tuple-element.130.refs_1_, ...), custom_call_target="tpu_custom_call" | custom-call | flops 1476395008 | bytes 6555676 | tf_op jit(solution)/shard_map/pallas_call | solution.py:339
  267.2 5.8 %shard_map.268 = bf16[1024,1920]{1,0:T(8,128)(2,1)} custom-call(s32[7]{0:T(128)} %stack.39.refs_0_, bf16[512,1024]{1,0:T(8,128)(2,1)} %get-tuple-element.105.refs_5_.refs_1_, bf16[512,768]{1,0:T(8,128)(2,1)} %get-tuple-element.149.refs_2_, bf16[1024,128]{1,0:T(8,128)(2,1)} %bitcast.28, bf16[128,1024]{1,0:T(8,128)(2,1)} %get-tuple-element.155.refs_4_, ...), custom_call_target="tpu_custom_call" | custom-call | flops 805306368 | bytes 7340060 | tf_op jit(solution)/shard_map/pallas_call | solution.py:339
  277.5 7.1 %collective-permute-done.27.refs_2_ = bf16[128,1024]{1,0:T(8,128)(2,1)S(1)} collective-permute-done((bf16[128,1024]{1,0:T(8,128)(2,1)S(1)}, bf16[128,1024]{1,0:T(8,128)(2,1)S(1)}, u32[]{:S(2)}, u32[]{:S(2)}) %collective-permute-start.27) | collective-permute-done | bytes 262176 | tf_op jit(solution)/shard_map/ppermute | solution.py:366
  284.6 8.9 %collective-permute-done.28.refs_3_ = bf16[128,1024]{1,0:T(8,128)(2,1)S(1)} collective-permute-done((bf16[128,1024]{1,0:T(8,128)(2,1)S(1)}, bf16[128,1024]{1,0:T(8,128)(2,1)S(1)}, u32[]{:S(2)}, u32[]{:S(2)}) %collective-permute-start.28) | collective-permute-done | bytes 262176 | tf_op jit(solution)/shard_map/ppermute | solution.py:366
  296.4 4.8 %collective-permute-start.31 = (bf16[32,2048]{1,0:T(8,128)(2,1)}, bf16[32,2048]{1,0:T(8,128)(2,1)S(1)}, u32[]{:S(2)}, u32[]{:S(2)}) collective-permute-start(bf16[32,2048]{1,0:T(8,128)(2,1)} %get-tuple-element.160), channel_id=1, source_target_pairs={{0,2},{2,0},{4,6},{6,4},{1,3},{3,1},{5,7},{7,5},{8,10},{10,8},{12,... | collective-permute-start | bytes 393224 | tf_op jit(solution)/shard_map/ppermute | solution.py:366
  306.3 18.5 %reduce-scatter.3.cloned.1.call-done.refs_1_ = bf16[128,1920]{1,0:T(8,128)(2,1)} async-done(((bf16[1024,1920]{1,0:T(8,128)(2,1)}), bf16[128,1920]{1,0:T(8,128)(2,1)}) %reduce-scatter.3.cloned.1.call-update) | async-done | bytes 491536 | tf_op jit(solution)/shard_map/reduce_scatter | solution.py:956
  337.2 4.8 %collective-permute-done.35.refs_3_ = bf16[32,1920]{1,0:T(8,128)(2,1)S(1)} collective-permute-done((bf16[32,1920]{1,0:T(8,128)(2,1)}, bf16[32,1920]{1,0:T(8,128)(2,1)S(1)}, u32[]{:S(2)}, u32[]{:S(2)}) %collective-permute-start.35) | collective-permute-done | bytes 122912 | tf_op jit(solution)/shard_map/ppermute | solution.py:366
  (201 shorter events, 86.9 us)
Async XLA Ops:
  7.2 70.2 %all-gather.3.cloned.1.call-start = ((), (), s32[]{:S(2)}) async-start(), calls=%async_computation.2 | async-start | bytes 1769472 | tf_op jit(solution)/shard_map/all_gather | solution.py:451
  27.4 89.1 %all-gather.5.cloned.1.call-start = ((), (), s32[]{:S(2)}) async-start(), calls=%async_computation.3 | async-start | bytes 9437184 | tf_op jit(solution)/shard_map/all_gather | solution.py:465
  27.6 16.4 %collective-permute-start.11 = (bf16[32,3072]{1,0:T(8,128)(2,1)}, bf16[32,3072]{1,0:T(8,128)(2,1)S(1)}, u32[]{:S(2)}, u32[]{:S(2)}) collective-permute-start(bf16[32,3072]{1,0:T(8,128)(2,1)} %get-tuple-element.108), channel_id=1, source_target_pairs={{0,4},{2,6},{4,0},{6,2},{1,5},{3,7},{5,1},{7,3},{8,12},{10,14},{12... | collective-permute-start | bytes 589832 | tf_op jit(solution)/shard_map/ppermute | solution.py:366
  28.8 15.2 %collective-permute-start.12 = (bf16[32,3072]{1,0:T(8,128)(2,1)}, bf16[32,3072]{1,0:T(8,128)(2,1)S(1)}, u32[]{:S(2)}, u32[]{:S(2)}) collective-permute-start(bf16[32,3072]{1,0:T(8,128)(2,1)} %get-tuple-element.109), channel_id=1, source_target_pairs={{0,6},{2,4},{4,2},{6,0},{1,7},{3,5},{5,3},{7,1},{8,14},{10,12},{12... | collective-permute-start | bytes 589832 | tf_op jit(solution)/shard_map/ppermute | solution.py:366
  47.2 246.3 %reduce-scatter.5.cloned.1.call-start = ((), (), s32[]{:S(2)}) async-start(), calls=%async_computation.5 | async-start | bytes 7077888 | tf_op jit(solution)/shard_map/reduce_scatter | solution.py:793
  48.8 16.9 %collective-permute-start.1 = (bf16[160,1024]{1,0:T(8,128)(2,1)S(1)}, bf16[160,1024]{1,0:T(8,128)(2,1)S(1)}, u32[]{:S(2)}, u32[]{:S(2)}) collective-permute-start(bf16[160,1024]{1,0:T(8,128)(2,1)S(1)} %constant_dynamic-update-slice_fusion.refs_1_.refs_8_), channel_id=1, source_target_pairs={{0,2},{2,0},{4,6},{6,4},{1,3},{3,1},{5,7},{7,5},{8,10},{10,8},{12,... | collective-permute-start | bytes 983048 | tf_op jit(solution)/shard_map/ppermute | solution.py:366
  51.9 25.5 %collective-permute-start.2 = (bf16[160,1024]{1,0:T(8,128)(2,1)S(1)}, bf16[160,1024]{1,0:T(8,128)(2,1)S(1)}, u32[]{:S(2)}, u32[]{:S(2)}) collective-permute-start(bf16[160,1024]{1,0:T(8,128)(2,1)S(1)} %constant_dynamic-update-slice_fusion.refs_1_.refs_8_), channel_id=1, source_target_pairs={{0,4},{2,6},{4,0},{6,2},{1,5},{3,7},{5,1},{7,3},{8,12},{10,14},{12... | collective-permute-start | bytes 983048 | tf_op jit(solution)/shard_map/ppermute | solution.py:366
  51.9 25.5 %collective-permute-start.3 = (bf16[160,1024]{1,0:T(8,128)(2,1)S(1)}, bf16[160,1024]{1,0:T(8,128)(2,1)S(1)}, u32[]{:S(2)}, u32[]{:S(2)}) collective-permute-start(bf16[160,1024]{1,0:T(8,128)(2,1)S(1)} %constant_dynamic-update-slice_fusion.refs_1_.refs_8_), channel_id=1, source_target_pairs={{0,6},{2,4},{4,2},{6,0},{1,7},{3,5},{5,3},{7,1},{8,14},{10,12},{12... | collective-permute-start | bytes 983048 | tf_op jit(solution)/shard_map/ppermute | solution.py:366
  88.5 16.8 %collective-permute-start.7 = (bf16[512,256]{1,0:T(8,128)(2,1)}, bf16[512,256]{1,0:T(8,128)(2,1)S(1)}, u32[]{:S(2)}, u32[]{:S(2)}) collective-permute-start(bf16[512,256]{1,0:T(8,128)(2,1)} %get-tuple-element.104.refs_1_.refs_5_), channel_id=1, source_target_pairs={{0,2},{2,0},{4,6},{6,4},{1,3},{3,1},{5,7},{7,5},{8,10},{10,8},{12,... | collective-permute-start | bytes 786440 | tf_op jit(solution)/shard_map/ppermute | solution.py:366
  95.0 21.6 %collective-permute-start.8 = (bf16[512,256]{1,0:T(8,128)(2,1)}, bf16[512,256]{1,0:T(8,128)(2,1)S(1)}, u32[]{:S(2)}, u32[]{:S(2)}) collective-permute-start(bf16[512,256]{1,0:T(8,128)(2,1)} %get-tuple-element.104.refs_1_.refs_5_), channel_id=1, source_target_pairs={{0,4},{2,6},{4,0},{6,2},{1,5},{3,7},{5,1},{7,3},{8,12},{10,14},{12... | collective-permute-start | bytes 786440 | tf_op jit(solution)/shard_map/ppermute | solution.py:366
  95.3 21.3 %collective-permute-start.9 = (bf16[512,256]{1,0:T(8,128)(2,1)}, bf16[512,256]{1,0:T(8,128)(2,1)S(1)}, u32[]{:S(2)}, u32[]{:S(2)}) collective-permute-start(bf16[512,256]{1,0:T(8,128)(2,1)} %get-tuple-element.104.refs_1_.refs_5_), channel_id=1, source_target_pairs={{0,6},{2,4},{4,2},{6,0},{1,7},{3,5},{5,3},{7,1},{8,14},{10,12},{12... | collective-permute-start | bytes 786440 | tf_op jit(solution)/shard_map/ppermute | solution.py:366
  131.4 13.7 %collective-permute-start.13 = (bf16[128,1024]{1,0:T(8,128)(2,1)}, bf16[128,1024]{1,0:T(8,128)(2,1)S(1)}, u32[]{:S(2)}, u32[]{:S(2)}) collective-permute-start(bf16[128,1024]{1,0:T(8,128)(2,1)} %get-tuple-element.113), channel_id=1, source_target_pairs={{0,2},{2,0},{4,6},{6,4},{1,3},{3,1},{5,7},{7,5},{8,10},{10,8},{12,... | collective-permute-start | bytes 786440 | tf_op jit(solution)/shard_map/ppermute | solution.py:366
  135.8 20.6 %collective-permute-start.14 = (bf16[128,1024]{1,0:T(8,128)(2,1)}, bf16[128,1024]{1,0:T(8,128)(2,1)S(1)}, u32[]{:S(2)}, u32[]{:S(2)}) collective-permute-start(bf16[128,1024]{1,0:T(8,128)(2,1)} %get-tuple-element.114), channel_id=1, source_target_pairs={{0,4},{2,6},{4,0},{6,2},{1,5},{3,7},{5,1},{7,3},{8,12},{10,14},{12... | collective-permute-start | bytes 786440 | tf_op jit(solution)/shard_map/ppermute | solution.py:366
  135.8 20.6 %collective-permute-start.15 = (bf16[128,1024]{1,0:T(8,128)(2,1)}, bf16[128,1024]{1,0:T(8,128)(2,1)S(1)}, u32[]{:S(2)}, u32[]{:S(2)}) collective-permute-start(bf16[128,1024]{1,0:T(8,128)(2,1)} %get-tuple-element.115), channel_id=1, source_target_pairs={{0,6},{2,4},{4,2},{6,0},{1,7},{3,5},{5,3},{7,1},{8,14},{10,12},{12... | collective-permute-start | bytes 786440 | tf_op jit(solution)/shard_map/ppermute | solution.py:366
  160.2 13.4 %collective-permute-start.18 = (bf16[128,1024]{1,0:T(8,128)(2,1)}, bf16[128,1024]{1,0:T(8,128)(2,1)S(1)}, u32[]{:S(2)}, u32[]{:S(2)}) collective-permute-start(bf16[128,1024]{1,0:T(8,128)(2,1)} %get-tuple-element.121.refs_1_), channel_id=1, source_target_pairs={{0,2},{2,0},{4,6},{6,4},{1,3},{3,1},{5,7},{7,5},{8,10},{10,8},{12,... | collective-permute-start | bytes 786440 | tf_op jit(solution)/shard_map/ppermute | solution.py:366
  164.3 20.2 %collective-permute-start.19 = (bf16[128,1024]{1,0:T(8,128)(2,1)}, bf16[128,1024]{1,0:T(8,128)(2,1)S(1)}, u32[]{:S(2)}, u32[]{:S(2)}) collective-permute-start(bf16[128,1024]{1,0:T(8,128)(2,1)} %get-tuple-element.121.refs_1_), channel_id=1, source_target_pairs={{0,4},{2,6},{4,0},{6,2},{1,5},{3,7},{5,1},{7,3},{8,12},{10,14},{12... | collective-permute-start | bytes 786440 | tf_op jit(solution)/shard_map/ppermute | solution.py:366
  164.3 20.2 %collective-permute-start.20 = (bf16[128,1024]{1,0:T(8,128)(2,1)}, bf16[128,1024]{1,0:T(8,128)(2,1)S(1)}, u32[]{:S(2)}, u32[]{:S(2)}) collective-permute-start(bf16[128,1024]{1,0:T(8,128)(2,1)} %get-tuple-element.121.refs_1_), channel_id=1, source_target_pairs={{0,6},{2,4},{4,2},{6,0},{1,7},{3,5},{5,3},{7,1},{8,14},{10,12},{12... | collective-permute-start | bytes 786440 | tf_op jit(solution)/shard_map/ppermute | solution.py:366
  207.6 117.3 %reduce-scatter.3.cloned.1.call-start = ((), (), s32[]{:S(2)}) async-start(), calls=%async_computation.4 | async-start | bytes 4423680 | tf_op jit(solution)/shard_map/reduce_scatter | solution.py:956
  208.4 13.1 %collective-permute-start.21 = (bf16[128,1024]{1,0:T(8,128)(2,1)S(1)}, bf16[128,1024]{1,0:T(8,128)(2,1)S(1)}, u32[]{:S(2)}, u32[]{:S(2)}) collective-permute-start(bf16[128,1024]{1,0:T(8,128)(2,1)S(1)} %copy-done.40), channel_id=1, source_target_pairs={{0,2},{2,0},{4,6},{6,4},{1,3},{3,1},{5,7},{7,5},{8,10},{10,8},{12,... | collective-permute-start | bytes 786440 | tf_op jit(solution)/shard_map/ppermute | solution.py:366
  212.8 20.4 %collective-permute-start.22 = (bf16[128,1024]{1,0:T(8,128)(2,1)S(1)}, bf16[128,1024]{1,0:T(8,128)(2,1)S(1)}, u32[]{:S(2)}, u32[]{:S(2)}) collective-permute-start(bf16[128,1024]{1,0:T(8,128)(2,1)S(1)} %copy-done.39), channel_id=1, source_target_pairs={{0,4},{2,6},{4,0},{6,2},{1,5},{3,7},{5,1},{7,3},{8,12},{10,14},{12... | collective-permute-start | bytes 786440 | tf_op jit(solution)/shard_map/ppermute | solution.py:366
  212.8 20.4 %collective-permute-start.23 = (bf16[128,1024]{1,0:T(8,128)(2,1)S(1)}, bf16[128,1024]{1,0:T(8,128)(2,1)S(1)}, u32[]{:S(2)}, u32[]{:S(2)}) collective-permute-start(bf16[128,1024]{1,0:T(8,128)(2,1)S(1)} %copy-done.38), channel_id=1, source_target_pairs={{0,6},{2,4},{4,2},{6,0},{1,7},{3,5},{5,3},{7,1},{8,14},{10,12},{12... | collective-permute-start | bytes 786440 | tf_op jit(solution)/shard_map/ppermute | solution.py:366
  273.1 11.5 %collective-permute-start.27 = (bf16[128,1024]{1,0:T(8,128)(2,1)S(1)}, bf16[128,1024]{1,0:T(8,128)(2,1)S(1)}, u32[]{:S(2)}, u32[]{:S(2)}) collective-permute-start(bf16[128,1024]{1,0:T(8,128)(2,1)S(1)} %copy-done.37), channel_id=1, source_target_pairs={{0,2},{2,0},{4,6},{6,4},{1,3},{3,1},{5,7},{7,5},{8,10},{10,8},{12,... | collective-permute-start | bytes 786440 | tf_op jit(solution)/shard_map/ppermute | solution.py:366
  274.3 19.2 %collective-permute-start.28 = (bf16[128,1024]{1,0:T(8,128)(2,1)S(1)}, bf16[128,1024]{1,0:T(8,128)(2,1)S(1)}, u32[]{:S(2)}, u32[]{:S(2)}) collective-permute-start(bf16[128,1024]{1,0:T(8,128)(2,1)S(1)} %copy-done.36), channel_id=1, source_target_pairs={{0,4},{2,6},{4,0},{6,2},{1,5},{3,7},{5,1},{7,3},{8,12},{10,14},{12... | collective-permute-start | bytes 786440 | tf_op jit(solution)/shard_map/ppermute | solution.py:366
  276.2 17.3 %collective-permute-start.29 = (bf16[128,1024]{1,0:T(8,128)(2,1)S(1)}, bf16[128,1024]{1,0:T(8,128)(2,1)S(1)}, u32[]{:S(2)}, u32[]{:S(2)}) collective-permute-start(bf16[128,1024]{1,0:T(8,128)(2,1)S(1)} %copy-done.35), channel_id=1, source_target_pairs={{0,6},{2,4},{4,2},{6,0},{1,7},{3,5},{5,3},{7,1},{8,14},{10,12},{12... | collective-permute-start | bytes 786440 | tf_op jit(solution)/shard_map/ppermute | solution.py:366
  296.4 28.4 %collective-permute-start.31 = (bf16[32,2048]{1,0:T(8,128)(2,1)}, bf16[32,2048]{1,0:T(8,128)(2,1)S(1)}, u32[]{:S(2)}, u32[]{:S(2)}) collective-permute-start(bf16[32,2048]{1,0:T(8,128)(2,1)} %get-tuple-element.160), channel_id=1, source_target_pairs={{0,2},{2,0},{4,6},{6,4},{1,3},{3,1},{5,7},{7,5},{8,10},{10,8},{12,... | collective-permute-start | bytes 393224 | tf_op jit(solution)/shard_map/ppermute | solution.py:366
  301.2 23.6 %collective-permute-start.32 = (bf16[32,2048]{1,0:T(8,128)(2,1)}, bf16[32,2048]{1,0:T(8,128)(2,1)S(1)}, u32[]{:S(2)}, u32[]{:S(2)}) collective-permute-start(bf16[32,2048]{1,0:T(8,128)(2,1)} %get-tuple-element.161), channel_id=1, source_target_pairs={{0,4},{2,6},{4,0},{6,2},{1,5},{3,7},{5,1},{7,3},{8,12},{10,14},{12... | collective-permute-start | bytes 393224 | tf_op jit(solution)/shard_map/ppermute | solution.py:366
  301.2 23.6 %collective-permute-start.33 = (bf16[32,2048]{1,0:T(8,128)(2,1)}, bf16[32,2048]{1,0:T(8,128)(2,1)S(1)}, u32[]{:S(2)}, u32[]{:S(2)}) collective-permute-start(bf16[32,2048]{1,0:T(8,128)(2,1)} %get-tuple-element.162), channel_id=1, source_target_pairs={{0,6},{2,4},{4,2},{6,0},{1,7},{3,5},{5,3},{7,1},{8,14},{10,12},{12... | collective-permute-start | bytes 393224 | tf_op jit(solution)/shard_map/ppermute | solution.py:366
  303.6 28.8 %collective-permute-start.17 = (bf16[64,1024]{1,0:T(8,128)(2,1)S(1)}, bf16[64,1024]{1,0:T(8,128)(2,1)S(1)}, u32[]{:S(2)}, u32[]{:S(2)}) collective-permute-start(bf16[64,1024]{1,0:T(8,128)(2,1)S(1)} %copy-done.45), channel_id=1, source_target_pairs={{0,1},{1,0},{2,3},{3,2},{4,5},{5,4},{6,7},{7,6},{8,9},{9,8},{10,11... | collective-permute-start | bytes 393224 | tf_op jit(solution)/shard_map/ppermute | solution.py:366
  305.8 28.9 %collective-permute-start.30 = (bf16[64,1024]{1,0:T(8,128)(2,1)}, bf16[64,1024]{1,0:T(8,128)(2,1)S(1)}, u32[]{:S(2)}, u32[]{:S(2)}) collective-permute-start(bf16[64,1024]{1,0:T(8,128)(2,1)} %get-tuple-element.148), channel_id=1, source_target_pairs={{0,1},{1,0},{2,3},{3,2},{4,5},{5,4},{6,7},{7,6},{8,9},{9,8},{10,11... | collective-permute-start | bytes 393224 | tf_op jit(solution)/shard_map/ppermute | solution.py:366
  328.0 9.2 %collective-permute-start.34 = (bf16[32,1920]{1,0:T(8,128)(2,1)}, bf16[32,1920]{1,0:T(8,128)(2,1)S(1)}, u32[]{:S(2)}, u32[]{:S(2)}) collective-permute-start(bf16[32,1920]{1,0:T(8,128)(2,1)} %get-tuple-element.164), channel_id=1, source_target_pairs={{0,2},{2,0},{4,6},{6,4},{1,3},{3,1},{5,7},{7,5},{8,10},{10,8},{12,... | collective-permute-start | bytes 368648 | tf_op jit(solution)/shard_map/ppermute | solution.py:366
  329.5 12.5 %collective-permute-start.35 = (bf16[32,1920]{1,0:T(8,128)(2,1)}, bf16[32,1920]{1,0:T(8,128)(2,1)S(1)}, u32[]{:S(2)}, u32[]{:S(2)}) collective-permute-start(bf16[32,1920]{1,0:T(8,128)(2,1)} %get-tuple-element.165), channel_id=1, source_target_pairs={{0,4},{2,6},{4,0},{6,2},{1,5},{3,7},{5,1},{7,3},{8,12},{10,14},{12... | collective-permute-start | bytes 368648 | tf_op jit(solution)/shard_map/ppermute | solution.py:366
  331.9 10.1 %collective-permute-start.36 = (bf16[32,1920]{1,0:T(8,128)(2,1)}, bf16[32,1920]{1,0:T(8,128)(2,1)S(1)}, u32[]{:S(2)}, u32[]{:S(2)}) collective-permute-start(bf16[32,1920]{1,0:T(8,128)(2,1)} %get-tuple-element.166), channel_id=1, source_target_pairs={{0,6},{2,4},{4,2},{6,0},{1,7},{3,5},{5,3},{7,1},{8,14},{10,12},{12... | collective-permute-start | bytes 368648 | tf_op jit(solution)/shard_map/ppermute | solution.py:366
  (58 other events, 360.5 us)
Sparse Core Ops, SparseCore 0:
  27.5 24.0 all-gather.2
  53.5 54.3 all-gather.4
  207.7 63.2 reduce-scatter.4
  274.7 50.0 reduce-scatter.2
